TPU v7x, 128 devices: a whole 4x4x4 slice. The times are simulated.
128 devices in a mesh: ctx: 8 (over y, z_lo), head: 16 (over z_hi, x, core).
Axes of the slice: x: 4, y: 4, z: 4 (z_hi: 2, z_lo: 2; z = z_hi * 2 + z_lo), core: 2. Of those that a mesh axis runs over, the one named last changes fastest.
Arguments:
- q_nope: bfloat16 [2048, 16384], P('ctx', 'head'), may hold values from -6 to 6
- q_rope: bfloat16 [2048, 8192], P('ctx', 'head'), may hold values from -6 to 6
- grad_out: bfloat16 [2048, 16384], P('ctx', 'head'), may hold values from -6 to 6
- kv_latent: bfloat16 [2048, 576], P('ctx'), may hold values from -6 to 6
- w_uk: bfloat16 [512, 16384], P(None, 'head'), may hold values from -0.5 to 0.5
- w_uv: bfloat16 [512, 16384], P(None, 'head'), may hold values from -0.25 to 0.25
- group_order: int32 [16], replicated, may hold values from 0 to 15, each once
Outputs:
- grad_q_nope: bfloat16 [2048, 16384], P('ctx', 'head')
- grad_q_rope: bfloat16 [2048, 8192], P('ctx', 'head')
- grad_kv: bfloat16 [2048, 576], P('ctx')
- grad_w_uk: float32 [512, 16384], P(None, 'head')
- grad_w_uv: float32 [512, 16384], P(None, 'head')
Inputs may be any that keep to these rules, and one draw needn't show every extreme that they name: `group_order`: each of the 16 sequence blocks appears once.
All inputs are finite; a program needn't handle non-finite values.
Results may differ from a plain program's by a relative error of at most 0.017.
Values may be sent and summed in bfloat16 or wider, within the bound.
No kernel may reach another device: no remote copies, remote signals or barrier semaphores. Data moves between devices by JAX's collectives and lax.ppermute only.
A program may use at most 64 MiB of HBM per device.

v0:
```python
import math

import jax
import jax.numpy as jnp
from jax import lax
from jax.sharding import PartitionSpec as P

NOPE = 128
ROPE = 64
VHEAD = 128
LATENT = 512


def head_terms(whole, visible, scale, q_h, r_h, g_h, uk_h, uv_h):
    values = whole[:, :LATENT]
    qa = jnp.dot(q_h, uk_h.T, preferred_element_type=jnp.float32).astype(jnp.bfloat16)
    q_full = jnp.concatenate([qa, r_h], axis=1)
    scores = jnp.dot(q_full, whole.T, preferred_element_type=jnp.float32) * scale
    scores = jnp.where(visible, scores, -jnp.inf)
    top = jnp.max(scores, axis=1, keepdims=True)
    expo = jnp.exp(scores - top)
    probs = expo / jnp.sum(expo, axis=1, keepdims=True)
    probs_b = probs.astype(jnp.bfloat16)
    out_lat = jnp.dot(probs_b, values, preferred_element_type=jnp.float32).astype(jnp.bfloat16)
    grad_lat = jnp.dot(g_h, uv_h.T, preferred_element_type=jnp.float32).astype(jnp.bfloat16)
    grad_probs = jnp.dot(grad_lat, values.T, preferred_element_type=jnp.float32)
    delta = jnp.sum(probs * grad_probs, axis=1, keepdims=True)
    grad_scores = (scale * probs * (grad_probs - delta)).astype(jnp.bfloat16)
    grad_qfull = jnp.dot(grad_scores, whole, preferred_element_type=jnp.float32)
    grad_qa = grad_qfull[:, :LATENT].astype(jnp.bfloat16)
    grad_rope = grad_qfull[:, LATENT:].astype(jnp.bfloat16)
    grad_nope = jnp.dot(grad_qa, uk_h, preferred_element_type=jnp.float32).astype(jnp.bfloat16)
    grad_wuk = jnp.dot(grad_qa.T, q_h, preferred_element_type=jnp.float32)
    grad_wuv = jnp.dot(out_lat.T, g_h, preferred_element_type=jnp.float32)
    score_part = jnp.dot(grad_scores.T, q_full, preferred_element_type=jnp.float32)
    value_part = jnp.dot(probs_b.T, grad_lat, preferred_element_type=jnp.float32)
    grad_keys = score_part + jnp.pad(value_part, ((0, 0), (0, ROPE)))
    return (grad_keys, (grad_nope, grad_rope, grad_wuk, grad_wuv))


def split_heads(array, count, width):
    return array.reshape(array.shape[0], count, width).transpose(1, 0, 2)


def join_heads(array):
    return array.transpose(1, 0, 2).reshape(array.shape[1], array.shape[0] * array.shape[2])


def on_device(q_nope, q_rope, grad_out, kv_latent, w_uk, w_uv, group_order):
    mscale = 0.1 * math.log(40.0) + 1.0
    scale = (NOPE + ROPE) ** (-0.5) * mscale * mscale
    rows = q_nope.shape[0]
    group = rows // 2
    local_heads = q_nope.shape[1] // NOPE
    whole = lax.all_gather(kv_latent, "ctx", axis=0, tiled=True)
    total = whole.shape[0]
    key_rows = jnp.arange(total, dtype=jnp.int32)
    slots = jnp.arange(group_order.shape[0], dtype=jnp.int32)
    owner = jnp.sum(
        jnp.where((key_rows // group)[:, None] == slots[None, :], group_order[None, :], 0), axis=1
    )
    key_pos = owner * group + key_rows % group
    query_pos = lax.dynamic_slice_in_dim(key_pos, lax.axis_index("ctx") * rows, rows)
    visible = query_pos[:, None] >= key_pos[None, :]

    def step(carry, items):
        grad_keys, outs = head_terms(whole, visible, scale, *items)
        return (carry + grad_keys, outs)

    items = (
        split_heads(q_nope, local_heads, NOPE),
        split_heads(q_rope, local_heads, ROPE),
        split_heads(grad_out, local_heads, VHEAD),
        split_heads(w_uk, local_heads, NOPE),
        split_heads(w_uv, local_heads, VHEAD),
    )
    partial_value, (g_nope, g_rope, g_uk, g_uv) = lax.scan(
        step, jnp.zeros((total, whole.shape[1]), jnp.float32), items
    )
    summed = lax.psum(partial_value, "head")
    grad_kv = lax.psum_scatter(summed, "ctx", scatter_dimension=0, tiled=True)
    sum_uk, sum_uv = (
        lax.psum(g_uk.astype(jnp.bfloat16), "ctx").astype(jnp.float32),
        lax.psum(g_uv.astype(jnp.bfloat16), "ctx").astype(jnp.float32),
    )
    return (
        join_heads(g_nope),
        join_heads(g_rope),
        grad_kv.astype(jnp.bfloat16),
        join_heads(sum_uk),
        join_heads(sum_uv),
    )


def solution(mesh):
    in_specs = (
        P("ctx", "head"),
        P("ctx", "head"),
        P("ctx", "head"),
        P("ctx", None),
        P(None, "head"),
        P(None, "head"),
        P(),
    )
    out_specs = (
        P("ctx", "head"),
        P("ctx", "head"),
        P("ctx", None),
        P(None, "head"),
        P(None, "head"),
    )
    return jax.shard_map(
        on_device, mesh=mesh, in_specs=in_specs, out_specs=out_specs, check_vma=False
    )
```

profile of v0, /device:TPU:0, one launch (start us, length us, event | category | flops | bytes accessed | tf_op | source)
XLA Modules:
  0.0 545.3 jit_solution(2184438112674807120)
XLA Ops:
  15.0 57.5 %all-gather.2.cloned.1.call-done = bf16[2048,576]{1,0:T(8,128)(2,1)} async-done(((bf16[256,576]{1,0:T(8,128)(2,1)}), bf16[2048,576]{1,0:T(8,128)(2,1)}) %all-gather.2.cloned.1.call-update) | async-done | bytes 2359312 | tf_op jit(solution)/shard_map/all_gather | solution.py:55
  72.5 177.7 %while.21 = (s32[]{:T(128)}, f32[2048,576]{0,1:T(8,128)}, bf16[8,256,128]{2,1,0:T(8,128)(2,1)}, bf16[8,256,64]{1,2,0:T(8,128)(2,1)}, bf16[8,512,128]{2,1,0:T(8,1...) while((s32[]{:T(128)}, f32[2048,576]{0,1:T(8,128)}, ...), condition=%wide.region_5.6_spmd.clone, body=%wide.region_1.5_spmd.clone.sunk | while | flops 3607149824 | bytes 109833616 | solution.py:77
  74.1 2.9 fusion.110
  77.4 3.3 fusion.116
  80.8 2.4 multiply_reduce_fusion.2
  96.3 2.9 fusion.110
  99.6 3.3 fusion.116
  118.5 2.9 fusion.110
  121.9 3.3 fusion.116
  140.7 2.9 fusion.110
  144.1 3.3 fusion.116
  162.9 2.9 fusion.110
  166.3 3.3 fusion.116
  185.2 2.9 fusion.110
  188.5 3.3 fusion.116
  207.4 2.9 fusion.110
  210.7 3.3 fusion.116
  229.6 2.9 fusion.110
  232.9 3.3 fusion.116
  250.1 3.3 copy_bitcast_fusion
  256.1 103.6 %all-reduce.5.cloned.1.call-done = (bf16[512,1024]{1,0:T(8,128)(2,1)}, bf16[512,1024]{1,0:T(8,128)(2,1)}) async-done(((bf16[512,1024]{1,0:T(8,128)(2,1)}, bf16[512,1024]{1,0:T(8,128)(2,1)}), (bf16[512,1024]{1,0:T(8,128)(2,1)}, bf16[512,1024]{1,0:T(8,128)(2,1)})) %all-reduce.5.cloned.1.call-update) | async-done | bytes 2097168 | tf_op jit(solution)/shard_map/psum | solution.py:83
  359.7 2.9 reshape.82
  364.2 98.2 %reduce-scatter.2.cloned.1.call-done = f32[256,576]{0,1:T(8,128)} async-done(((f32[2048,576]{0,1:T(8,128)}), f32[256,576]{0,1:T(8,128)}) %reduce-scatter.2.cloned.1.call-update) | async-done | bytes 589840 | tf_op jit(solution)/shard_map/reduce_scatter | solution.py:81
  462.4 76.4 %all-reduce.6 = bf16[256,576]{0,1:T(8,128)(2,1)} all-reduce(f32[256,576]{0,1:T(8,128)} %reduce-scatter.2.cloned.1.call-done), channel_id=1, replica_groups=mesh['ctx'=8,'head'=16] {'head'}, use_global_device_ids=true, to_apply=%region_6.7 | all-reduce | flops 147456 | bytes 884736 | tf_op jit(solution)/shard_map/psum | solution.py:80
  (275 shorter events, 136.7 us)
Async XLA Ops:
  7.2 4.5 copy-start.7
  7.2 5.5 %copy-start.6 = (bf16[512,1024]{1,0:T(8,128)(2,1)S(1)}, bf16[512,1024]{1,0:T(8,128)(2,1)}, u32[]{:S(2)}) copy-start(bf16[512,1024]{1,0:T(8,128)(2,1)} %param.13) | copy-start | bytes 3145732
  7.2 65.3 %all-gather.2.cloned.1.call-start = ((), (), s32[]{:S(2)}) async-start(), calls=%async_computation.1 | async-start | bytes 2949120 | tf_op jit(solution)/shard_map/all_gather | solution.py:55
  9.2 350.5 %all-reduce.5.cloned.1.call-start = ((), (), s32[]{:S(2)}) async-start(), calls=%async_computation.3 | async-start | bytes 4194304 | tf_op jit(solution)/shard_map/psum | solution.py:83
  91.0 3.6 copy-start.2
  91.0 3.6 copy-start.4
  110.7 2.2 slice-start
  113.2 3.6 copy-start.2
  113.2 3.6 copy-start.4
  132.9 2.2 slice-start
  135.4 3.6 copy-start.2
  135.5 3.6 copy-start.4
  157.7 3.6 copy-start.2
  157.7 3.6 copy-start.4
  179.9 3.6 copy-start.2
  179.9 3.6 copy-start.4
  202.1 3.6 copy-start.2
  202.1 3.6 copy-start.4
  224.3 3.6 copy-start.2
  224.3 3.6 copy-start.4
  246.5 3.6 copy-start.2
  246.5 3.6 copy-start.4
  253.4 209.0 %reduce-scatter.2.cloned.1.call-start = ((), (), s32[]{:S(2)}) async-start(), calls=%async_computation.2 | async-start | bytes 5308416 | tf_op jit(solution)/shard_map/reduce_scatter | solution.py:81
  359.7 2.9 copy-start.5
  (49 other events, 84.5 us)
Sparse Core Ops, SparseCore 0:
  9.7 62.7 all-gather.1
  253.5 106.1 all-reduce.4
  362.2 100.2 reduce-scatter.1
where the time goes:
time: 548 us; the launch traced here: 545 us
  waiting for transfers between devices  260 us (47%)
  matrix products  130 us (24%)
  blocking collectives  76.4 us (14%)
  local copies, waits for them, and re-layouts  50.8 us (9%)
  between operations  13.9 us (3%)
  other arithmetic  13.5 us (2%)
    psum x1, waiting for transfers between devices, on_device(): lax.psum(g_uk.astype(jnp.bfloat16), 'ctx').astype(jnp.float32)  104 us
    reduce_scatter x1, waiting for transfers between devices, on_device(): grad_kv = lax.psum_scatter(summed, 'ctx', scatter_dimension=0, tiled=True)  98.2 us
    psum x1, blocking collectives, on_device(): summed = lax.psum(partial_value, 'head')  76.4 us
    all_gather x1, waiting for transfers between devices, on_device(): whole = lax.all_gather(kv_latent, 'ctx', axis=0, tiled=True)  57.5 us
    while x128, local copies, waits for them, and re-layouts  32.2 us
    dot_general x8, matrix products, head_terms(): grad_wuv = jnp.dot(out_lat.T, g_h, preferred_element_type=jnp.float32)  26.6 us
    dot_general x8, matrix products, head_terms(): jnp.dot(q_full, whole.T, preferred_element_type=jnp.float32) * scale  23.1 us
    dot_general x8, matrix products, head_terms(): grad_probs = jnp.dot(grad_lat, values.T, preferred_element_type=jnp.float32)  19.5 us
  transfers between devices with their start and end apart: 3, of which 3 were waited for; matrix products, arithmetic and copies ran while one was open for 2% of the time, Pallas kernels for 0%

commit v1 on v0

v1 whole, which is shorter than its diff:
```python
import functools
import math

import jax
import jax.numpy as jnp
from jax import lax
from jax.experimental import pallas as pl
from jax.experimental.pallas import tpu as pltpu
from jax.sharding import PartitionSpec as P

NOPE = 128
ROPE = 64
VHEAD = 128
LATENT = 512
GROUP = 128
GROUPS = 16
TOKENS = GROUP * GROUPS
CTX = 8
HEAD = 16
MSCALE = 0.1 * math.log(40.0) + 1.0
SCALE = (NOPE + ROPE) ** (-0.5) * MSCALE * MSCALE
BLOCK = 256
F32 = jnp.float32
BF16 = jnp.bfloat16
VMEM = pl.BlockSpec(memory_space=pltpu.VMEM)
SMEM = pl.BlockSpec(memory_space=pltpu.SMEM)
PARAMS = pltpu.CompilerParams(vmem_limit_bytes=56 * 1024 * 1024)

Q0, G0, R0, K0, KR0, CHUNK = 0, 256, 512, 640, 1152, 1216


def nt(a, b):
    return lax.dot_general(a, b, (((1,), (1,)), ((), ())), preferred_element_type=F32)


def nn(a, b):
    return jnp.dot(a, b, preferred_element_type=F32)


def pack_kernel(core, q, r, g, kv, send):
    half = kv[pl.ds(pl.multiple_of(core[0] * GROUP, GROUP), GROUP), :]
    for i in range(CTX):
        send[i, Q0:Q0 + 256, :] = q[:, i * 128:(i + 1) * 128]
        send[i, G0:G0 + 256, :] = g[:, i * 128:(i + 1) * 128]
        rope = r[:, i * ROPE:(i + 1) * ROPE]
        send[i, R0:R0 + 128, :] = jnp.concatenate([rope[:128], rope[128:]], axis=1)
        for j in range(4):
            send[i, K0 + 128 * j:K0 + 128 * (j + 1), :] = half[:, 128 * j:128 * (j + 1)]
        tail = half[:, LATENT:]
        send[i, KR0:KR0 + 64, :] = jnp.concatenate([tail[:64], tail[64:]], axis=1)


def pack(core, q, r, g, kv):
    return pl.pallas_call(
        pack_kernel,
        out_shape=jax.ShapeDtypeStruct((CTX, CHUNK, 128), BF16),
        in_specs=[SMEM, VMEM, VMEM, VMEM, VMEM],
        out_specs=VMEM,
        compiler_params=PARAMS,
        name="pack",
    )(core, q, r, g, kv)


def head_kernel(order, core, recv, other, uk, uv, send, guk, guv,
                val, qf, go, kf, kt, vf, gk, gv, gq):
    def gather(p, carry):
        s = order[p]
        c, b = s // 2, s % 2
        rows = pl.ds(pl.multiple_of(p * GROUP, GROUP), GROUP)
        shift = pl.multiple_of(b * GROUP, GROUP)
        qf[rows, :NOPE] = recv[c, pl.ds(Q0 + shift, GROUP), :]
        go[rows, :] = recv[c, pl.ds(G0 + shift, GROUP), :]
        pair = recv[c, R0:R0 + 128, :]
        qf[rows, NOPE:] = jnp.where(b == 0, pair[:, :ROPE], pair[:, ROPE:])

        def take(ref, base):
            for j in range(4):
                val[rows, 128 * j:128 * (j + 1)] = ref[c, base + 128 * j:base + 128 * (j + 1), :]
            tail = ref[c, base + 512:base + 576, :]
            kf[rows, NOPE:] = jnp.concatenate([tail[:, :ROPE], tail[:, ROPE:]], axis=0)

        @pl.when(b == core[0])
        def _():
            take(recv, K0)

        @pl.when(b != core[0])
        def _():
            take(other, 0)

        return carry

    lax.fori_loop(0, GROUPS, gather, 0)

    ukt = jnp.transpose(uk[...].astype(F32)).astype(BF16)
    for p in range(TOKENS // BLOCK):
        rows = slice(p * BLOCK, (p + 1) * BLOCK)
        latent = val[rows, :]
        kf[rows, :NOPE] = nn(latent, uk[...]).astype(BF16)
        vf[rows, :] = nn(latent, uv[...]).astype(BF16)
        kt[:NOPE, rows] = nt(ukt, latent).astype(BF16)
        kt[NOPE:, rows] = jnp.transpose(kf[rows, NOPE:].astype(F32)).astype(BF16)

    factor = SCALE * math.log2(math.e)
    key_at = lax.broadcasted_iota(jnp.int32, (BLOCK, BLOCK), 0)
    query_at = lax.broadcasted_iota(jnp.int32, (BLOCK, BLOCK), 1)
    seen = key_at <= query_at
    for i in range(TOKENS // BLOCK):
        mine = slice(i * BLOCK, (i + 1) * BLOCK)
        q_i, g_i = qf[mine, :], go[mine, :]
        scores = []
        for j in range(i + 1):
            s = nt(kf[j * BLOCK:(j + 1) * BLOCK, :], q_i) * factor
            if j == i:
                s = jnp.where(seen, s, -jnp.inf)
            scores.append(s)
        top = functools.reduce(jnp.maximum, [jnp.max(s, axis=0, keepdims=True) for s in scores])
        expo = [jnp.exp2(s - top) for s in scores]
        total = functools.reduce(jnp.add, [jnp.sum(e, axis=0, keepdims=True) for e in expo])
        inverse = 1.0 / total
        grads = [nt(vf[j * BLOCK:(j + 1) * BLOCK, :], g_i) for j in range(i + 1)]
        delta = functools.reduce(
            jnp.add, [jnp.sum(e * d, axis=0, keepdims=True) for e, d in zip(expo, grads)]
        ) * inverse
        acc = None
        for j in range(i + 1):
            rows = slice(j * BLOCK, (j + 1) * BLOCK)
            probs = expo[j] * inverse
            ds = (probs * (grads[j] - delta)).astype(BF16)
            part = nn(kt[:, rows], ds)
            acc = part if acc is None else acc + part
            to_k = nn(ds, q_i)
            to_v = nn(probs.astype(BF16), g_i)
            if j == i:
                gk[rows, :] = to_k
                gv[rows, :] = to_v
            else:
                gk[rows, :] += to_k
                gv[rows, :] += to_v
        gq[mine, :] = jnp.transpose(acc) * SCALE

    uk_sum = uv_sum = None
    for p in range(TOKENS // BLOCK):
        rows = slice(p * BLOCK, (p + 1) * BLOCK)
        latent = val[rows, :]
        kp = nn(jnp.transpose(gk[rows, :NOPE] * SCALE).astype(BF16), latent)
        vp = nn(jnp.transpose(gv[rows, :]).astype(BF16), latent)
        uk_sum = kp if uk_sum is None else uk_sum + kp
        uv_sum = vp if uv_sum is None else uv_sum + vp
    guk[...] = jnp.transpose(uk_sum).astype(BF16)
    guv[...] = jnp.transpose(uv_sum).astype(BF16)

    def scatter(p, carry):
        s = order[p]
        c, b = s // 2, s % 2
        rows = pl.ds(pl.multiple_of(p * GROUP, GROUP), GROUP)
        to = pl.ds(pl.multiple_of(b * GROUP, GROUP), GROUP)
        send[c, to, :128] = gq[rows, :NOPE].astype(BF16)
        send[c, to, 128:256] = (gk[rows, :NOPE] * SCALE).astype(BF16)
        send[c, to, 256:384] = gv[rows, :].astype(BF16)
        send[c, to, 384:512] = jnp.concatenate(
            [gq[rows, NOPE:], gk[rows, NOPE:] * SCALE], axis=1
        ).astype(BF16)
        return carry

    lax.fori_loop(0, GROUPS, scatter, 0)


def head_call(order, core, recv, other, uk, uv):
    return pl.pallas_call(
        head_kernel,
        out_shape=(
            jax.ShapeDtypeStruct((CTX, 256, 512), BF16),
            jax.ShapeDtypeStruct((LATENT, NOPE), BF16),
            jax.ShapeDtypeStruct((LATENT, VHEAD), BF16),
        ),
        in_specs=[SMEM, SMEM, VMEM, VMEM, VMEM, VMEM],
        out_specs=(VMEM, VMEM, VMEM),
        scratch_shapes=[
            pltpu.VMEM((TOKENS, LATENT), BF16),
            pltpu.VMEM((TOKENS, NOPE + ROPE), BF16),
            pltpu.VMEM((TOKENS, VHEAD), BF16),
            pltpu.VMEM((TOKENS, NOPE + ROPE), BF16),
            pltpu.VMEM((NOPE + ROPE, TOKENS), BF16),
            pltpu.VMEM((TOKENS, VHEAD), BF16),
            pltpu.VMEM((TOKENS, NOPE + ROPE), F32),
            pltpu.VMEM((TOKENS, VHEAD), F32),
            pltpu.VMEM((TOKENS, NOPE + ROPE), F32),
        ],
        compiler_params=PARAMS,
        name="head",
    )(order, core, recv, other, uk, uv)


def post_kernel(core, back, uk, uv, gqn, gqr, own, away):
    acc = None
    rope = None
    for i in range(CTX):
        cols = slice(i * 128, (i + 1) * 128)
        gqn[:, cols] = back[i, :, :128]
        gqr[:, i * ROPE:(i + 1) * ROPE] = back[i, :, 384:448]
        part = nt(back[i, :, 128:256], uk[:, cols]) + nt(back[i, :, 256:384], uv[:, cols])
        tail = back[i, :, 448:].astype(F32)
        acc = part if acc is None else acc + part
        rope = tail if rope is None else rope + tail
    low = core[0] == 0
    own[:, :LATENT] = jnp.where(low, acc[:128], acc[128:])
    own[:, LATENT:] = jnp.where(low, rope[:128], rope[128:])
    away[:, :LATENT] = jnp.where(low, acc[128:], acc[:128]).astype(BF16)
    away[:, LATENT:] = jnp.where(low, rope[128:], rope[:128]).astype(BF16)


def post(core, back, uk, uv):
    width = LATENT + ROPE
    return pl.pallas_call(
        post_kernel,
        out_shape=(
            jax.ShapeDtypeStruct((256, 1024), BF16),
            jax.ShapeDtypeStruct((256, 512), BF16),
            jax.ShapeDtypeStruct((128, width), F32),
            jax.ShapeDtypeStruct((128, width), BF16),
        ),
        in_specs=[SMEM, VMEM, VMEM, VMEM],
        out_specs=(VMEM, VMEM, VMEM, VMEM),
        compiler_params=PARAMS,
        name="post",
    )(core, back, uk, uv)


def spread(array, axis, groups=None, count=CTX):
    copies = jnp.broadcast_to(array[None], (count,) + array.shape)
    return lax.all_to_all(copies, axis, 0, 0, tiled=True, axis_index_groups=groups)


def on_device(q_nope, q_rope, grad_out, kv_latent, w_uk, w_uv, group_order):
    slots = jnp.arange(GROUPS, dtype=jnp.int32)
    order = jnp.sum(jnp.where(group_order[None, :] == slots[:, None], slots[None, :], 0), axis=1)
    mine = lax.axis_index("ctx")
    core = (lax.axis_index("head") % 2).astype(jnp.int32)[None]
    swap = [(i, i ^ 1) for i in range(HEAD)]
    lanes = [[c + 2 * k for k in range(CTX)] for c in range(2)]

    sent = pack(core, q_nope, q_rope, grad_out, kv_latent)
    recv = lax.all_to_all(sent, "ctx", 0, 0, tiled=True)
    other = lax.ppermute(recv[:, K0:, :], "head", swap)
    uk_h = lax.dynamic_slice_in_dim(w_uk, mine * NOPE, NOPE, 1)
    uv_h = lax.dynamic_slice_in_dim(w_uv, mine * VHEAD, VHEAD, 1)
    back, guk, guv = head_call(order, core, recv, other, uk_h, uv_h)
    back = lax.all_to_all(back, "ctx", 0, 0, tiled=True)
    grads = spread(jnp.concatenate([guk, guv], axis=0), "ctx")
    gqn, gqr, own, away = post(core, back, w_uk, w_uv)
    pair = (own + lax.ppermute(away, "head", swap).astype(F32)).astype(BF16)
    total = jnp.sum(spread(pair, "head", lanes).astype(F32), axis=0).astype(BF16)
    peer = lax.ppermute(total, "head", swap)
    low = core[0] == 0
    grad_kv = jnp.concatenate(
        [jnp.where(low, total, peer), jnp.where(low, peer, total)], axis=0
    )
    wide = grads.astype(F32)
    sum_uk = wide[:, :LATENT].transpose(1, 0, 2).reshape(LATENT, CTX * NOPE)
    sum_uv = wide[:, LATENT:].transpose(1, 0, 2).reshape(LATENT, CTX * VHEAD)
    return gqn, gqr, grad_kv, sum_uk, sum_uv


def solution(mesh):
    in_specs = (
        P("ctx", "head"),
        P("ctx", "head"),
        P("ctx", "head"),
        P("ctx", None),
        P(None, "head"),
        P(None, "head"),
        P(),
    )
    out_specs = (
        P("ctx", "head"),
        P("ctx", "head"),
        P("ctx", None),
        P(None, "head"),
        P(None, "head"),
    )
    return jax.shard_map(
        on_device, mesh=mesh, in_specs=in_specs, out_specs=out_specs, check_vma=False
    )
```

time: 548 us -> 176 us (0.32)
  waiting for transfers between devices: 260 us -> 72.4 us
  matrix products: 130 us -> 0 us
  blocking collectives: 76.4 us -> 37.1 us
  local copies, waits for them, and re-layouts: 50.8 us -> 18.5 us
  Pallas kernels: 0 us -> 27.8 us
  starting transfers between devices: 0.12 us -> 14.8 us
  between operations: 13.9 us -> 0.73 us
  other arithmetic: 13.5 us -> 2.64 us
    dot_general x80 -> x0, matrix products: 130 us -> none  [the longest x8 26.6 us: head_terms(): grad_wuv = jnp.dot(out_lat.T, g_h, preferred_element_type=jnp.float32)]
    psum x1 -> x0, waiting for transfers between devices: 104 us -> none  [on_device(): lax.psum(g_uk.astype(jnp.bfloat16), 'ctx').astype(jnp.float32)]
    reduce_scatter x1 -> x0, waiting for transfers between devices: 98.2 us -> none  [on_device(): grad_kv = lax.psum_scatter(summed, 'ctx', scatter_dimension=0, tiled=True)]
    psum x1 -> x0, blocking collectives: 76.4 us -> none  [on_device(): summed = lax.psum(partial_value, 'head')]
    all_to_all x0 -> x3, waiting for transfers between devices: none -> 70 us  [the longest x2 38.1 us: spread(): lax.all_to_all(copies, axis, 0, 0, tiled=True, axis_index_groups=groups)]
    all_gather x1 -> x0, waiting for transfers between devices: 57.5 us -> none  [on_device(): whole = lax.all_gather(kv_latent, 'ctx', axis=0, tiled=True)]
    all_to_all x0 -> x1, blocking collectives: none -> 37.1 us  [on_device(): recv = lax.all_to_all(sent, 'ctx', 0, 0, tiled=True)]
    while x128 -> x0, local copies, waits for them, and re-layouts: 32.2 us -> none
  transfers between devices with their start and end apart: 3 -> 6, of which waited for: 3 -> 5; matrix products, arithmetic and copies ran while one was open for 2% -> 8% of each run, Pallas kernels for 0% -> 3%
where the time goes in v1:
time: 176 us; the launch traced here: 174 us
  waiting for transfers between devices  72.4 us (41%)
  blocking collectives  37.1 us (21%)
  Pallas kernels  27.8 us (16%)
  local copies, waits for them, and re-layouts  18.5 us (11%)
  starting transfers between devices  14.8 us (8%)
  other arithmetic  2.64 us (2%)
    all_to_all x2, waiting for transfers between devices, spread(): lax.all_to_all(copies, axis, 0, 0, tiled=True, axis_index_groups=groups)  38.1 us
    all_to_all x1, blocking collectives, on_device(): recv = lax.all_to_all(sent, 'ctx', 0, 0, tiled=True)  37.1 us
    all_to_all x1, waiting for transfers between devices, on_device(): back = lax.all_to_all(back, 'ctx', 0, 0, tiled=True)  31.9 us
    pallas_call x1, Pallas kernels, head_call(): pl.pallas_call(head_kernel, out_shape=(jax.ShapeDtypeStruct((CTX, 256, 51...  20.2 us
    all_to_all x2, starting transfers between devices, spread(): lax.all_to_all(copies, axis, 0, 0, tiled=True, axis_index_groups=groups)  11 us
    unnamed x17, local copies, waits for them, and re-layouts  6.96 us
    pallas_call x1, Pallas kernels, post(): pl.pallas_call(post_kernel, out_shape=(jax.ShapeDtypeStruct((256, 1024),...  4.43 us
    all_to_all x1, starting transfers between devices, on_device(): back = lax.all_to_all(back, 'ctx', 0, 0, tiled=True)  3.74 us
  transfers between devices with their start and end apart: 6, of which 5 were waited for; matrix products, arithmetic and copies ran while one was open for 8% of the time, Pallas kernels for 3%

profile of v1, /device:TPU:0, one launch (start us, length us, event | category | flops | bytes accessed | tf_op | source)
XLA Modules:
  0.0 174.1 jit_solution(3657641376936040038)
XLA Ops:
  0.6 1.9 %copy.20.kv = bf16[256,576]{1,0:T(8,128)(2,1)} copy(bf16[256,576]{0,1:T(8,128)(2,1)} %param.10) | data formatting | bytes 589824 | tf_op args[3]
  2.5 3.2 %pack.1 = bf16[8,1216,128]{2,1,0:T(8,128)(2,1)} custom-call(s32[1]{0:T(128)} %bitcast.core, bf16[256,1024]{1,0:T(8,128)(2,1)} %q.1, bf16[256,512]{1,0:T(8,128)(2,1)} %r.1, bf16[256,1024]{1,0:T(8,128)(2,1)} %g.1, bf16[256,576]{1,0:T(8,128)(2,1)} %copy.20.kv), custom_call_target="tpu_custom_call" | custom-call | tf_op jit(solution)/shard_map/pack/pallas_call | solution.py:54
  5.7 37.1 %all_to_all.20.recv = bf16[8,1216,128]{2,1,0:T(8,128)(2,1)S(1)} all-to-all(bf16[8,1216,128]{2,1,0:T(8,128)(2,1)} %pack.1), channel_id=1, replica_groups=mesh['ctx'=8,'head'=16] {'ctx'}, dimensions={0} | all-to-all | bytes 4980736 | tf_op jit(solution)/shard_map/all_to_all | solution.py:243
  42.9 1.2 slice.12
  44.1 0.7 select_reduce_fusion.order
  44.7 1.7 constant_dynamic-slice_fusion
  46.4 0.8 collective-permute-done.other
  47.3 20.2 %head.1 = (bf16[8,256,512]{2,1,0:T(8,128)(2,1)}, bf16[512,128]{1,0:T(8,128)(2,1)}, bf16[512,128]{1,0:T(8,128)(2,1)}) custom-call(s32[16]{0:T(128)} %select_reduce_fusion.order, s32[1]{0:T(128)} %bitcast.core, bf16[8,1216,128]{2,1,0:T(8,128)(2,1)} %copy-done, bf16[8,576,128]{2,1,0:T(8,128)(2,1)} %collective-permute-done.other, ...), custom_call_target="tpu_custom_call" | custom-call | tf_op jit(solution)/shard_map/head/pallas_call | solution.py:169
  67.4 3.7 %all-to-all-start.1 = ((bf16[8,256,512]{2,1,0:T(8,128)(2,1)}), bf16[8,256,512]{2,1,0:T(8,128)(2,1)S(1)}, u32[]{:S(2)}, u32[]{:S(2)}) async-start(bf16[8,256,512]{2,1,0:T(8,128)(2,1)} %get-tuple-element.12), calls=%async_computation.1 | async-start | bytes 4194304 | tf_op jit(solution)/shard_map/all_to_all | solution.py:248
  71.2 31.9 %all-to-all-done.1.back = bf16[8,256,512]{2,1,0:T(8,128)(2,1)S(1)} async-done(((bf16[8,256,512]{2,1,0:T(8,128)(2,1)}), bf16[8,256,512]{2,1,0:T(8,128)(2,1)S(1)}, u32[]{:S(2)}, u32[]{:S(2)}) %all-to-all-start.1) | async-done | bytes 2097184 | tf_op jit(solution)/shard_map/all_to_all | solution.py:248
  103.1 1.8 %broadcast_in_dim.34 = bf16[8,1024,128]{2,1,0:T(8,128)(2,1)} broadcast(bf16[1024,128]{1,0:T(8,128)(2,1)S(1)} %pad_maximum_fusion.1), dimensions={1,2} | broadcast | bytes 2359296 | tf_op jit(solution)/shard_map/broadcast_in_dim | solution.py:230
  105.1 3.6 %all-to-all-start.3 = ((bf16[8,1024,128]{2,1,0:T(8,128)(2,1)}), bf16[8,1024,128]{2,1,0:T(8,128)(2,1)S(1)}, u32[]{:S(2)}, u32[]{:S(2)}) async-start(bf16[8,1024,128]{2,1,0:T(8,128)(2,1)} %broadcast_in_dim.34), calls=%async_computation.3 | async-start | bytes 4194304 | tf_op jit(solution)/shard_map/all_to_all | solution.py:231
  108.7 4.4 %post.1 = (bf16[256,1024]{1,0:T(8,128)(2,1)}, bf16[256,512]{1,0:T(8,128)(2,1)}, f32[128,576]{1,0:T(8,128)}, bf16[128,576]{1,0:T(8,128)(2,1)}) custom-call(s32[1]{0:T(128)} %bitcast.core, bf16[8,256,512]{2,1,0:T(8,128)(2,1)} %copy-done.2, bf16[512,1024]{1,0:T(8,128)(2,1)} %uk.1, bf16[512,1024]{1,0:T(8,128)(2,1)} %uv.1), custom_call_target="tpu_custom_call" | custom-call | tf_op jit(solution)/shard_map/post/pallas_call | solution.py:214
  113.2 1.6 collective-permute-done.1
  114.8 1.0 add_convert_fusion
  115.9 23.4 %all-to-all-done.3 = bf16[8,1024,128]{2,1,0:T(8,128)(2,1)S(1)} async-done(((bf16[8,1024,128]{2,1,0:T(8,128)(2,1)}), bf16[8,1024,128]{2,1,0:T(8,128)(2,1)S(1)}, u32[]{:S(2)}, u32[]{:S(2)}) %all-to-all-start.3) | async-done | bytes 2097184 | tf_op jit(solution)/shard_map/all_to_all | solution.py:231
  139.4 1.3 broadcast_in_dim.33
  140.6 7.4 %all-to-all-start.2 = ((bf16[8,128,576]{1,2,0:T(8,128)(2,1)}), bf16[8,128,576]{1,2,0:T(8,128)(2,1)S(1)}, u32[]{:S(2)}, u32[]{:S(2)}) async-start(bf16[8,128,576]{1,2,0:T(8,128)(2,1)} %broadcast_in_dim.33), calls=%async_computation.2 | async-start | bytes 2359296 | tf_op jit(solution)/shard_map/all_to_all | solution.py:231
  148.0 2.9 %copy.22 = bf16[8,1024,128]{1,2,0:T(8,128)(2,1)S(1)} copy(bf16[8,1024,128]{2,1,0:T(8,128)(2,1)} %copy-done.1) | data formatting | bytes 4194304 | tf_op jit(solution)/shard_map/all_to_all | solution.py:231
  150.9 14.7 %all-to-all-done.2 = bf16[8,128,576]{1,2,0:T(8,128)(2,1)S(1)} async-done(((bf16[8,128,576]{1,2,0:T(8,128)(2,1)}), bf16[8,128,576]{1,2,0:T(8,128)(2,1)S(1)}, u32[]{:S(2)}, u32[]{:S(2)}) %all-to-all-start.2) | async-done | bytes 1179680 | tf_op jit(solution)/shard_map/all_to_all | solution.py:231
  165.8 2.6 %fusion = (f32[8,512,128]{1,2,0:T(8,128)}, f32[8,512,128]{1,2,0:T(8,128)}) fusion(bf16[8,1024,128]{1,2,0:T(8,128)(2,1)S(1)} %copy.22), kind=kLoop, calls=%fused_computation.9 | loop fusion | bytes 8388608 | tf_op jit(solution)/shard_map/slice | solution.py:260
  168.4 3.0 %copy.24 = f32[512,1024]{1,0:T(8,128)} copy(f32[512,1024]{0,1:T(8,128)} %bitcast.8) | data formatting | bytes 4194304
  171.5 1.8 %copy.23 = f32[512,1024]{1,0:T(8,128)} copy(f32[512,1024]{0,1:T(8,128)S(1)} %bitcast.7) | data formatting | bytes 4194304
  173.3 0.7 pad_maximum_fusion
  (22 shorter events, 0.7 us)
Async XLA Ops:
  42.9 4.4 %copy-start = (bf16[8,1216,128]{2,1,0:T(8,128)(2,1)}, bf16[8,1216,128]{2,1,0:T(8,128)(2,1)S(1)}, u32[]{:S(2)}) copy-start(bf16[8,1216,128]{2,1,0:T(8,128)(2,1)S(1)} %all_to_all.20.recv) | copy-start | bytes 7471108
  42.9 1.2 copy-start.6
  44.1 3.2 %collective-permute-start = (bf16[8,576,128]{2,1,0:T(8,128)(2,1)}, bf16[8,576,128]{2,1,0:T(8,128)(2,1)}, u32[]{:S(2)}, u32[]{:S(2)}) collective-permute-start(bf16[8,576,128]{2,1,0:T(8,128)(2,1)} %slice.12), channel_id=1, source_target_pairs={{0,1},{1,0},{2,3},{3,2},{4,5},{5,4},{6,7},{7,6},{8,9},{9,8},{10,11... | collective-permute-start | bytes 3538952 | tf_op jit(solution)/shard_map/ppermute | solution.py:244
  67.4 3.8 %copy-start.4 = (bf16[512,128]{1,0:T(8,128)(2,1)S(1)}, bf16[512,128]{1,0:T(8,128)(2,1)}, u32[]{:S(2)}) copy-start(bf16[512,128]{1,0:T(8,128)(2,1)} %get-tuple-element.17) | copy-start | bytes 393220
  67.4 3.8 %copy-start.5 = (bf16[512,128]{1,0:T(8,128)(2,1)S(1)}, bf16[512,128]{1,0:T(8,128)(2,1)}, u32[]{:S(2)}) copy-start(bf16[512,128]{1,0:T(8,128)(2,1)} %get-tuple-element.18) | copy-start | bytes 393220
  67.4 35.7 %all-to-all-start.1 = ((bf16[8,256,512]{2,1,0:T(8,128)(2,1)}), bf16[8,256,512]{2,1,0:T(8,128)(2,1)S(1)}, u32[]{:S(2)}, u32[]{:S(2)}) async-start(bf16[8,256,512]{2,1,0:T(8,128)(2,1)} %get-tuple-element.12), calls=%async_computation.1 | async-start | bytes 4194304 | tf_op jit(solution)/shard_map/all_to_all | solution.py:248
  103.1 2.0 %copy-start.2 = (bf16[8,256,512]{2,1,0:T(8,128)(2,1)}, bf16[8,256,512]{2,1,0:T(8,128)(2,1)S(1)}, u32[]{:S(2)}) copy-start(bf16[8,256,512]{2,1,0:T(8,128)(2,1)S(1)} %all-to-all-done.1.back) | copy-start | bytes 6291460
  105.1 34.2 %all-to-all-start.3 = ((bf16[8,1024,128]{2,1,0:T(8,128)(2,1)}), bf16[8,1024,128]{2,1,0:T(8,128)(2,1)S(1)}, u32[]{:S(2)}, u32[]{:S(2)}) async-start(bf16[8,1024,128]{2,1,0:T(8,128)(2,1)} %broadcast_in_dim.34), calls=%async_computation.3 | async-start | bytes 4194304 | tf_op jit(solution)/shard_map/all_to_all | solution.py:231
  113.2 1.6 collective-permute-start.1
  139.3 8.6 %copy-start.1 = (bf16[8,1024,128]{2,1,0:T(8,128)(2,1)}, bf16[8,1024,128]{2,1,0:T(8,128)(2,1)S(1)}, u32[]{:S(2)}) copy-start(bf16[8,1024,128]{2,1,0:T(8,128)(2,1)S(1)} %all-to-all-done.3) | copy-start | bytes 6291460
  140.6 24.9 %all-to-all-start.2 = ((bf16[8,128,576]{1,2,0:T(8,128)(2,1)}), bf16[8,128,576]{1,2,0:T(8,128)(2,1)S(1)}, u32[]{:S(2)}, u32[]{:S(2)}) async-start(bf16[8,128,576]{1,2,0:T(8,128)(2,1)} %broadcast_in_dim.33), calls=%async_computation.2 | async-start | bytes 2359296 | tf_op jit(solution)/shard_map/all_to_all | solution.py:231
  165.7 7.6 %collective-permute-start.2 = (bf16[128,576]{0,1:T(8,128)(2,1)S(1)}, bf16[128,576]{0,1:T(8,128)(2,1)S(1)}, u32[]{:S(2)}, u32[]{:S(2)}) collective-permute-start(bf16[128,576]{0,1:T(8,128)(2,1)S(1)} %reduce_sum.22), channel_id=1, source_target_pairs={{0,1},{1,0},{2,3},{3,2},{4,5},{5,4},{6,7},{7,6},{8,9},{9,8},{10,11... | collective-permute-start | bytes 442376 | tf_op jit(solution)/shard_map/ppermute | solution.py:253
  168.4 3.0 %copy-start.3 = (f32[8,512,128]{1,2,0:T(8,128)S(1)}, f32[8,512,128]{1,2,0:T(8,128)}, u32[]{:S(2)}) copy-start(f32[8,512,128]{1,2,0:T(8,128)} %get-tuple-element.30) | copy-start | bytes 6291460

commit v2 on v1

v2 whole, which is shorter than its diff:
```python
import functools
import math

import jax
import jax.numpy as jnp
from jax import lax
from jax.experimental import pallas as pl
from jax.experimental.pallas import tpu as pltpu
from jax.sharding import PartitionSpec as P

NOPE = 128
ROPE = 64
VHEAD = 128
LATENT = 512
WIDTH = LATENT + ROPE
GROUP = 128
GROUPS = 16
TOKENS = GROUP * GROUPS
CTX = 8
HEAD = 16
MSCALE = 0.1 * math.log(40.0) + 1.0
SCALE = (NOPE + ROPE) ** (-0.5) * MSCALE * MSCALE
BLOCK = 256
BLOCKS = TOKENS // BLOCK
F32 = jnp.float32
BF16 = jnp.bfloat16
VMEM = pl.BlockSpec(memory_space=pltpu.VMEM)
SMEM = pl.BlockSpec(memory_space=pltpu.SMEM)
PARAMS = pltpu.CompilerParams(vmem_limit_bytes=56 * 1024 * 1024)


def nt(a, b):
    return lax.dot_general(a, b, (((1,), (1,)), ((), ())), preferred_element_type=F32)


def nn(a, b):
    return jnp.dot(a, b, preferred_element_type=F32)


def pack_kernel(q, r, g, send):
    for i in range(CTX):
        send[i, :256, :] = q[:, i * 128:(i + 1) * 128]
        send[i, 256:512, :] = g[:, i * 128:(i + 1) * 128]
        rope = r[:, i * ROPE:(i + 1) * ROPE]
        send[i, 512:, :] = jnp.concatenate([rope[:128], rope[128:]], axis=1)


def pack(q, r, g):
    return pl.pallas_call(
        pack_kernel,
        out_shape=jax.ShapeDtypeStruct((CTX, 640, 128), BF16),
        in_specs=[VMEM, VMEM, VMEM],
        out_specs=VMEM,
        compiler_params=PARAMS,
        name="pack",
    )(q, r, g)


def head_kernel(order, place, recv, *refs):
    latents, (uk, uv, keys, rest, val, qf, go, kf, kt, vf, gk, gv, gq) = refs[:8], refs[8:]
    me, core = place[0], place[1]
    y, z = me // 2, lax.rem(me, 2)

    def at(s):
        return pl.ds(pl.multiple_of(order[s] * GROUP, GROUP), GROUP)

    for dy in range(4):
        for rc in range(2):
            for rz in range(2):
                c = lax.rem(y + dy, 4) * 2 + lax.rem(z + rz, 2)
                cols = at(c * 2 + lax.rem(core + rc, 2))
                src = latents[dy * 2 + rc]
                val[:, cols] = src[rz, :LATENT, :]
                kt[NOPE:, cols] = src[rz, LATENT:, :]
    for s in range(GROUPS):
        c, b = s // 2, s % 2
        rows = at(s)
        qf[rows, :NOPE] = recv[c, b * 128:(b + 1) * 128, :]
        go[rows, :] = recv[c, 256 + b * 128:256 + (b + 1) * 128, :]
        qf[rows, NOPE:] = recv[c, 512:640, b * ROPE:(b + 1) * ROPE]

    ukt = jnp.transpose(uk[...].astype(F32)).astype(BF16)
    uvt = jnp.transpose(uv[...].astype(F32)).astype(BF16)
    for p in range(BLOCKS):
        rows = slice(p * BLOCK, (p + 1) * BLOCK)
        latent = val[:, rows]
        k_t = nn(ukt, latent)
        kt[:NOPE, rows] = k_t.astype(BF16)
        kf[rows, :NOPE] = jnp.transpose(k_t).astype(BF16)
        kf[rows, NOPE:] = jnp.transpose(kt[NOPE:, rows].astype(F32)).astype(BF16)
        vf[rows, :] = jnp.transpose(nn(uvt, latent)).astype(BF16)

    factor = SCALE * math.log2(math.e)
    key_at = lax.broadcasted_iota(jnp.int32, (BLOCK, BLOCK), 0)
    query_at = lax.broadcasted_iota(jnp.int32, (BLOCK, BLOCK), 1)
    seen = key_at <= query_at
    for i in range(BLOCKS):
        mine = slice(i * BLOCK, (i + 1) * BLOCK)
        q_i, g_i = qf[mine, :], go[mine, :]
        scores = []
        for j in range(i + 1):
            s = nt(kf[j * BLOCK:(j + 1) * BLOCK, :], q_i) * factor
            if j == i:
                s = jnp.where(seen, s, -jnp.inf)
            scores.append(s)
        top = functools.reduce(jnp.maximum, [jnp.max(s, axis=0, keepdims=True) for s in scores])
        expo = [jnp.exp2(s - top) for s in scores]
        total = functools.reduce(jnp.add, [jnp.sum(e, axis=0, keepdims=True) for e in expo])
        inverse = 1.0 / total
        grads = [nt(vf[j * BLOCK:(j + 1) * BLOCK, :], g_i) for j in range(i + 1)]
        delta = functools.reduce(
            jnp.add, [jnp.sum(e * d, axis=0, keepdims=True) for e, d in zip(expo, grads)]
        ) * inverse
        acc = None
        for j in range(i + 1):
            rows = slice(j * BLOCK, (j + 1) * BLOCK)
            probs = expo[j] * inverse
            ds = (probs * (grads[j] - delta)).astype(BF16)
            part = nn(kt[:, rows], ds)
            acc = part if acc is None else acc + part
            to_k = nn(ds, q_i)
            to_v = nn(probs.astype(BF16), g_i)
            if j == i:
                gk[rows, :] = to_k
                gv[rows, :] = to_v
            else:
                gk[rows, :] += to_k
                gv[rows, :] += to_v
        gq[mine, :] = jnp.transpose(acc) * SCALE

    gkb = (gk[...] * SCALE).astype(BF16)
    gvb = gv[...].astype(BF16)
    guk = nn(val[...], gkb[:, :NOPE]).astype(BF16)
    guv = nn(val[...], gvb).astype(BF16)
    kf[...] = gkb
    vf[...] = gvb
    for c in range(CTX):
        rest[c, 384:896, :] = guk
        rest[c, 896:, :] = guv
        lo, hi = at(2 * c), at(2 * c + 1)
        keys[c, :128, :] = kf[lo, :NOPE]
        keys[c, 128:256, :] = kf[hi, :NOPE]
        keys[c, 256:384, :] = vf[lo, :]
        keys[c, 384:512, :] = vf[hi, :]
        keys[c, 512:, :] = jnp.concatenate([kf[lo, NOPE:], kf[hi, NOPE:]], axis=1)
        first, second = gq[lo, :], gq[hi, :]
        rest[c, :128, :] = first[:, :NOPE].astype(BF16)
        rest[c, 128:256, :] = second[:, :NOPE].astype(BF16)
        rest[c, 256:384, :] = jnp.concatenate(
            [first[:, NOPE:], second[:, NOPE:]], axis=1
        ).astype(BF16)


def head_call(order, place, recv, latents, uk, uv):
    whole = lambda shape: pl.BlockSpec(shape, lambda t, o, m: (0,) * len(shape))
    column = pl.BlockSpec((LATENT, NOPE), lambda t, o, m: (0, m[0]))
    return pl.pallas_call(
        head_kernel,
        out_shape=(
            jax.ShapeDtypeStruct((CTX, 640, 128), BF16),
            jax.ShapeDtypeStruct((CTX, 1408, 128), BF16),
        ),
        grid_spec=pltpu.PrefetchScalarGridSpec(
            num_scalar_prefetch=2,
            grid=(1,),
            in_specs=[whole((CTX, 640, 128))] + [whole((2, WIDTH, 128))] * 8 + [column, column],
            out_specs=(whole((CTX, 640, 128)), whole((CTX, 1408, 128))),
            scratch_shapes=[
                pltpu.VMEM((LATENT, TOKENS), BF16),
                pltpu.VMEM((TOKENS, NOPE + ROPE), BF16),
                pltpu.VMEM((TOKENS, VHEAD), BF16),
                pltpu.VMEM((TOKENS, NOPE + ROPE), BF16),
                pltpu.VMEM((NOPE + ROPE, TOKENS), BF16),
                pltpu.VMEM((TOKENS, VHEAD), BF16),
                pltpu.VMEM((TOKENS, NOPE + ROPE), F32),
                pltpu.VMEM((TOKENS, VHEAD), F32),
                pltpu.VMEM((TOKENS, NOPE + ROPE), F32),
            ],
        ),
        compiler_params=PARAMS,
        name="head",
    )(order, place, recv, *latents, uk, uv)


def post_kernel(place, back, uk, uv, own, away):
    acc = rope = None
    for i in range(CTX):
        cols = slice(i * 128, (i + 1) * 128)
        part = nt(uk[:, cols], back[i, :256, :]) + nt(uv[:, cols], back[i, 256:512, :])
        tail = back[i, 512:, :].astype(F32)
        acc = part if acc is None else acc + part
        rope = tail if rope is None else rope + tail
    turned = jnp.transpose(rope)
    low = place[1] == 0
    own[:LATENT, :] = jnp.where(low, acc[:, :128], acc[:, 128:])
    own[LATENT:, :] = jnp.where(low, turned[:ROPE], turned[ROPE:])
    away[:LATENT, :] = jnp.where(low, acc[:, 128:], acc[:, :128]).astype(BF16)
    away[LATENT:, :] = jnp.where(low, turned[ROPE:], turned[:ROPE]).astype(BF16)


def post(place, back, uk, uv):
    return pl.pallas_call(
        post_kernel,
        out_shape=(
            jax.ShapeDtypeStruct((WIDTH, 128), F32),
            jax.ShapeDtypeStruct((WIDTH, 128), BF16),
        ),
        in_specs=[SMEM, VMEM, VMEM, VMEM],
        out_specs=(VMEM, VMEM),
        compiler_params=PARAMS,
        name="post",
    )(place, back, uk, uv)


def finish_kernel(rest, gqn, gqr, guk, guv):
    for t in range(2):
        cols = slice(128 * t, 128 * (t + 1))
        gqn[:, cols] = rest[t, :256, :]
        pair = rest[t, 256:384, :]
        gqr[:128, ROPE * t:ROPE * (t + 1)] = pair[:, :ROPE]
        gqr[128:, ROPE * t:ROPE * (t + 1)] = pair[:, ROPE:]
        guk[:, cols] = rest[t, 384:896, :].astype(F32)
        guv[:, cols] = rest[t, 896:, :].astype(F32)


def finish(rest):
    return pl.pallas_call(
        finish_kernel,
        out_shape=(
            jax.ShapeDtypeStruct((256, 1024), BF16),
            jax.ShapeDtypeStruct((256, 512), BF16),
            jax.ShapeDtypeStruct((LATENT, 1024), F32),
            jax.ShapeDtypeStruct((LATENT, 1024), F32),
        ),
        grid=(4,),
        in_specs=[pl.BlockSpec((2, 1408, 128), lambda t: (t, 0, 0))],
        out_specs=(
            pl.BlockSpec((256, 256), lambda t: (0, t)),
            pl.BlockSpec((256, 128), lambda t: (0, t)),
            pl.BlockSpec((LATENT, 256), lambda t: (0, t)),
            pl.BlockSpec((LATENT, 256), lambda t: (0, t)),
        ),
        compiler_params=PARAMS,
        name="finish",
    )(rest)


CORE_SWAP = [(i, i ^ 1) for i in range(HEAD)]
ZLO_SWAP = [(i, i ^ 1) for i in range(CTX)]
ZHI_SWAP = [(i, i ^ 8) for i in range(HEAD)]


def from_y(step):
    return [(((c // 2 + step) % 4) * 2 + c % 2, c) for c in range(CTX)]


def from_x(step):
    return [((h & 8) + ((h // 2 + step) % 4) * 2 + h % 2, h) for h in range(HEAD)]


def gather_latent(half):
    near = jnp.stack([half, lax.ppermute(half, "ctx", ZLO_SWAP)])
    found = [near] + [lax.ppermute(near, "ctx", from_y(d)) for d in (1, 2, 3)]
    return [part for f in found for part in (f, lax.ppermute(f, "head", CORE_SWAP))]


def sum_heads(own, away):
    pair = (own + lax.ppermute(away, "head", CORE_SWAP).astype(F32)).astype(BF16)
    one, two, three = (lax.ppermute(pair, "head", from_x(d)).astype(F32) for d in (1, 2, 3))
    quad = ((pair.astype(F32) + two) + (one + three)).astype(BF16)
    far = lax.ppermute(quad, "head", ZHI_SWAP)
    return (quad.astype(F32) + far.astype(F32)).astype(BF16)


def on_device(q_nope, q_rope, grad_out, kv_latent, w_uk, w_uv, group_order):
    core = lax.axis_index("head") % 2
    place = jnp.stack([lax.axis_index("ctx"), core]).astype(jnp.int32)
    half = lax.dynamic_slice_in_dim(kv_latent.T, core * GROUP, GROUP, 1)
    latents = gather_latent(half)
    recv = lax.all_to_all(pack(q_nope, q_rope, grad_out), "ctx", 0, 0, tiled=True)
    keys, rest = head_call(group_order, place, recv, latents, w_uk, w_uv)
    keys = lax.all_to_all(keys, "ctx", 0, 0, tiled=True)
    keys, rest = lax.optimization_barrier((keys, rest))
    rest = lax.all_to_all(rest, "ctx", 0, 0, tiled=True)
    total = sum_heads(*post(place, keys, w_uk, w_uv))
    peer = lax.ppermute(total, "head", CORE_SWAP)
    low = core == 0
    grad_kv = jnp.concatenate(
        [jnp.where(low, total, peer), jnp.where(low, peer, total)], axis=1
    ).T
    gqn, gqr, guk, guv = finish(rest)
    return gqn, gqr, grad_kv, guk, guv


def solution(mesh):
    in_specs = (
        P("ctx", "head"),
        P("ctx", "head"),
        P("ctx", "head"),
        P("ctx", None),
        P(None, "head"),
        P(None, "head"),
        P(),
    )
    out_specs = (
        P("ctx", "head"),
        P("ctx", "head"),
        P("ctx", None),
        P(None, "head"),
        P(None, "head"),
    )
    return jax.shard_map(
        on_device, mesh=mesh, in_specs=in_specs, out_specs=out_specs, check_vma=False
    )
```

time: 176 us -> 140 us (0.80)
  waiting for transfers between devices: 72.4 us -> 55.7 us
  local copies, waits for them, and re-layouts: 18.5 us -> 2.81 us
  blocking collectives: 37.1 us -> 23.1 us
  starting transfers between devices: 14.8 us -> 26.7 us
    all_to_all x3 -> x2, waiting for transfers between devices: 70 us -> 1.84 us  [the longest x1 1.84 us: on_device(): rest = lax.all_to_all(rest, 'ctx', 0, 0, tiled=True)]
    ppermute x3 -> x14, waiting for transfers between devices: 2.44 us -> 53.9 us  [the longest x1 17.4 us: gather_latent(): near = jnp.stack([half, lax.ppermute(half, 'ctx', ZLO_SWAP)])]
    ppermute x3 -> x14, starting transfers between devices: 0.09 us -> 17.1 us  [the longest x3 5.67 us: gather_latent(): found = [near] + [lax.ppermute(near, 'ctx', from_y(d)) for d in (1, 2, 3)]]
    all_to_all x1, blocking collectives: 37.1 us -> 23.1 us  [on_device(): keys = lax.all_to_all(keys, 'ctx', 0, 0, tiled=True)]
    all_to_all x3 -> x2, starting transfers between devices: 14.7 us -> 9.55 us  [the longest x1 5.91 us: on_device(): lax.all_to_all(pack(q_nope, q_rope, grad_out), 'ctx', 0, 0, tiled=True)]
    unnamed x17 -> x20, local copies, waits for them, and re-layouts: 6.96 us -> 2.78 us
    slice x2 -> x0, local copies, waits for them, and re-layouts: 3.82 us -> none  [the longest x1 2.63 us: on_device(): sum_uv = wide[:, LATENT:].transpose(1, 0, 2).reshape(LATENT, CTX * VHEAD)]
    broadcast_in_dim x2 -> x0, local copies, waits for them, and re-layouts: 3.05 us -> none  [spread(): copies = jnp.broadcast_to(array[None], (count,) + array.shape)]
  transfers between devices with their start and end apart: 6 -> 16, of which waited for: 5 -> 12; matrix products, arithmetic and copies ran while one was open for 8% -> 2% of each run, Pallas kernels for 3% -> 3%
where the time goes in v2:
time: 140 us
  waiting for transfers between devices  55.7 us (40%)
  Pallas kernels  28.2 us (20%)
  starting transfers between devices  26.7 us (19%)
  blocking collectives  23.1 us (16%)
  local copies, waits for them, and re-layouts  2.81 us (2%)
  other arithmetic  2.56 us (2%)
    all_to_all x1, blocking collectives, on_device(): keys = lax.all_to_all(keys, 'ctx', 0, 0, tiled=True)  23.1 us
    ppermute x1, waiting for transfers between devices, gather_latent(): near = jnp.stack([half, lax.ppermute(half, 'ctx', ZLO_SWAP)])  17.4 us
    pallas_call x1, Pallas kernels, head_call(): pl.pallas_call(head_kernel, out_shape=(jax.ShapeDtypeStruct((CTX, 640, 12...  17.1 us
    ppermute x1, waiting for transfers between devices, sum_heads(): far = lax.ppermute(quad, 'head', ZHI_SWAP)  15.5 us
    ppermute x3, waiting for transfers between devices, gather_latent(): found = [near] + [lax.ppermute(near, 'ctx', from_y(d)) for d in (1, 2, 3)]  10.8 us
    ppermute x3, waiting for transfers between devices, sum_heads(): lax.ppermute(pair, 'head', from_x(d)).astype(F32)  6.21 us
    all_to_all x1, starting transfers between devices, on_device(): lax.all_to_all(pack(q_nope, q_rope, grad_out), 'ctx', 0, 0, tiled=True)  5.91 us
    ppermute x3, starting transfers between devices, gather_latent(): found = [near] + [lax.ppermute(near, 'ctx', from_y(d)) for d in (1, 2, 3)]  5.67 us
  transfers between devices with their start and end apart: 16, of which 12 were waited for; matrix products, arithmetic and copies ran while one was open for 2% of the time, Pallas kernels for 3%

profile of v2, /device:TPU:0, one launch (start us, length us, event | category | flops | bytes accessed | tf_op | source)
XLA Modules:
  0.0 139.8 jit_solution(16643989587097559949)
XLA Ops:
  0.6 2.6 %pack.1 = bf16[8,640,128]{2,1,0:T(8,128)(2,1)} custom-call(bf16[256,1024]{1,0:T(8,128)(2,1)} %q.1, bf16[256,512]{1,0:T(8,128)(2,1)} %r.1, bf16[256,1024]{1,0:T(8,128)(2,1)} %g.1), custom_call_target="tpu_custom_call" | custom-call | tf_op jit(solution)/shard_map/pack/pallas_call | solution.py:49
  3.3 5.9 %all-to-all-start = ((bf16[8,640,128]{2,1,0:T(8,128)(2,1)}), bf16[8,640,128]{2,1,0:T(8,128)(2,1)S(1)}, u32[]{:S(2)}, u32[]{:S(2)}) async-start(bf16[8,640,128]{2,1,0:T(8,128)(2,1)} %pack.1), calls=%async_computation | async-start | bytes 2621440 | tf_op jit(solution)/shard_map/all_to_all | solution.py:280
  9.2 2.1 %collective-permute-start = (bf16[576,128]{1,0:T(8,128)(2,1)S(1)}, bf16[576,128]{1,0:T(8,128)(2,1)S(1)}, u32[]{:S(2)}, u32[]{:S(2)}) collective-permute-start(bf16[576,128]{1,0:T(8,128)(2,1)S(1)} %get-tuple-element.28), channel_id=1, source_target_pairs={{0,16},{16,0},{32,48},{48,32},{64,80},{80,64},{96,112},{112,96},{1... | collective-permute-start | bytes 442376 | tf_op jit(solution)/shard_map/ppermute | solution.py:262
  11.3 17.4 %collective-permute-done = bf16[576,128]{1,0:T(8,128)(2,1)S(1)} collective-permute-done((bf16[576,128]{1,0:T(8,128)(2,1)S(1)}, bf16[576,128]{1,0:T(8,128)(2,1)S(1)}, u32[]{:S(2)}, u32[]{:S(2)}) %collective-permute-start) | collective-permute-done | bytes 147488 | tf_op jit(solution)/shard_map/ppermute | solution.py:262
  28.8 1.5 %collective-permute-start.6 = (bf16[2,576,128]{2,1,0:T(8,128)(2,1)S(1)}, bf16[2,576,128]{2,1,0:T(8,128)(2,1)S(1)}, u32[]{:S(2)}, u32[]{:S(2)}) collective-permute-start(bf16[2,576,128]{2,1,0:T(8,128)(2,1)S(1)} %pad_maximum_fusion.refs_0_), channel_id=1, source_target_pairs={{96,0},{112,16},{0,32},{16,48},{32,64},{48,80},{64,96},{80,112},{9... | collective-permute-start | bytes 884744 | tf_op jit(solution)/shard_map/ppermute | solution.py:263
  30.3 2.7 %collective-permute-start.4 = (bf16[2,576,128]{2,1,0:T(8,128)(2,1)S(1)}, bf16[2,576,128]{2,1,0:T(8,128)(2,1)S(1)}, u32[]{:S(2)}, u32[]{:S(2)}) collective-permute-start(bf16[2,576,128]{2,1,0:T(8,128)(2,1)S(1)} %pad_maximum_fusion.refs_0_), channel_id=1, source_target_pairs={{64,0},{80,16},{96,32},{112,48},{0,64},{16,80},{32,96},{48,112},{6... | collective-permute-start | bytes 884744 | tf_op jit(solution)/shard_map/ppermute | solution.py:263
  33.0 1.5 %collective-permute-start.2 = (bf16[2,576,128]{2,1,0:T(8,128)(2,1)S(1)}, bf16[2,576,128]{2,1,0:T(8,128)(2,1)S(1)}, u32[]{:S(2)}, u32[]{:S(2)}) collective-permute-start(bf16[2,576,128]{2,1,0:T(8,128)(2,1)S(1)} %pad_maximum_fusion.refs_0_), channel_id=1, source_target_pairs={{32,0},{48,16},{64,32},{80,48},{96,64},{112,80},{0,96},{16,112},{3... | collective-permute-start | bytes 884744 | tf_op jit(solution)/shard_map/ppermute | solution.py:263
  34.5 4.0 %collective-permute-done.6.refs_6_ = bf16[2,576,128]{2,1,0:T(8,128)(2,1)S(1)} collective-permute-done((bf16[2,576,128]{2,1,0:T(8,128)(2,1)S(1)}, bf16[2,576,128]{2,1,0:T(8,128)(2,1)S(1)}, u32[]{:S(2)}, u32[]{:S(2)}) %collective-permute-start.6) | collective-permute-done | bytes 294944 | tf_op jit(solution)/shard_map/ppermute | solution.py:263
  38.4 6.9 %collective-permute-done.4.refs_4_ = bf16[2,576,128]{2,1,0:T(8,128)(2,1)S(1)} collective-permute-done((bf16[2,576,128]{2,1,0:T(8,128)(2,1)S(1)}, bf16[2,576,128]{2,1,0:T(8,128)(2,1)S(1)}, u32[]{:S(2)}, u32[]{:S(2)}) %collective-permute-start.4) | collective-permute-done | bytes 294944 | tf_op jit(solution)/shard_map/ppermute | solution.py:263
  48.7 17.1 %head.1 = (bf16[8,640,128]{2,1,0:T(8,128)(2,1)}, bf16[8,1408,128]{2,1,0:T(8,128)(2,1)}) custom-call(s32[16]{0:T(128)} %order.1, s32[2]{0:T(128)} %pad_add_fusion.place, bf16[8,640,128]{2,1,0:T(8,128)(2,1)} %copy-done.1, bf16[2,576,128]{2,1,0:T(8,128)(2,1)} %copy-done.2, bf16[2,576,128]{2,1,0:T(8,128)(2,1)} %copy-done.6, bf16[2,576,128]{2,1,0:T(8,128)(2,1)} %copy-done.5, ...), custom_call_target="tpu_custom_call" | custom-call | tf_op jit(solution)/shard_map/head/pallas_call | solution.py:157
  65.7 23.1 %all_to_all.15.back = bf16[8,640,128]{2,1,0:T(8,128)(2,1)} all-to-all(bf16[8,640,128]{2,1,0:T(8,128)(2,1)} %get-tuple-element.15), channel_id=1, replica_groups=mesh['ctx'=8,'head'=16] {'ctx'}, dimensions={0} | all-to-all | bytes 2621440 | tf_op jit(solution)/shard_map/all_to_all | solution.py:282
  88.8 3.6 %all-to-all-start.2 = ((bf16[8,1408,128]{2,1,0:T(8,128)(2,1)}), bf16[8,1408,128]{2,1,0:T(8,128)(2,1)S(1)}, u32[]{:S(2)}, u32[]{:S(2)}) async-start(bf16[8,1408,128]{2,1,0:T(8,128)(2,1)} %get-tuple-element.17), calls=%async_computation.2 | async-start | bytes 5767168 | tf_op jit(solution)/shard_map/all_to_all | solution.py:284
  92.4 3.9 %post.1 = (f32[576,128]{1,0:T(8,128)}, bf16[576,128]{1,0:T(8,128)(2,1)}) custom-call(s32[2]{0:T(128)} %pad_add_fusion.place, bf16[8,640,128]{2,1,0:T(8,128)(2,1)} %all_to_all.15.back, bf16[512,1024]{1,0:T(8,128)(2,1)} %uk.1, bf16[512,1024]{1,0:T(8,128)(2,1)} %uv.1), custom_call_target="tpu_custom_call" | custom-call | tf_op jit(solution)/shard_map/post/pallas_call | solution.py:202
  96.4 1.6 %collective-permute-done.8 = bf16[576,128]{1,0:T(8,128)(2,1)S(1)} collective-permute-done((bf16[576,128]{1,0:T(8,128)(2,1)}, bf16[576,128]{1,0:T(8,128)(2,1)S(1)}, u32[]{:S(2)}, u32[]{:S(2)}) %collective-permute-start.8) | collective-permute-done | bytes 147488 | tf_op jit(solution)/shard_map/ppermute | solution.py:268
  99.0 1.6 %collective-permute-start.11 = (bf16[576,128]{1,0:T(8,128)(2,1)S(1)}, bf16[576,128]{1,0:T(8,128)(2,1)S(1)}, u32[]{:S(2)}, u32[]{:S(2)}) collective-permute-start(bf16[576,128]{1,0:T(8,128)(2,1)S(1)} %add_convert_fusion.2), channel_id=1, source_target_pairs={{6,0},{7,1},{0,2},{1,3},{2,4},{3,5},{4,6},{5,7},{14,8},{15,9},{8,1... | collective-permute-start | bytes 442376 | tf_op jit(solution)/shard_map/ppermute | solution.py:269
  100.5 1.7 %collective-permute-start.10 = (bf16[576,128]{1,0:T(8,128)(2,1)S(1)}, bf16[576,128]{1,0:T(8,128)(2,1)S(1)}, u32[]{:S(2)}, u32[]{:S(2)}) collective-permute-start(bf16[576,128]{1,0:T(8,128)(2,1)S(1)} %add_convert_fusion.2), channel_id=1, source_target_pairs={{2,0},{3,1},{4,2},{5,3},{6,4},{7,5},{0,6},{1,7},{10,8},{11,9},{12,... | collective-permute-start | bytes 442376 | tf_op jit(solution)/shard_map/ppermute | solution.py:269
  102.3 1.8 %collective-permute-start.9 = (bf16[576,128]{1,0:T(8,128)(2,1)S(1)}, bf16[576,128]{1,0:T(8,128)(2,1)S(1)}, u32[]{:S(2)}, u32[]{:S(2)}) collective-permute-start(bf16[576,128]{1,0:T(8,128)(2,1)S(1)} %add_convert_fusion.2), channel_id=1, source_target_pairs={{4,0},{5,1},{6,2},{7,3},{0,4},{1,5},{2,6},{3,7},{12,8},{13,9},{14,... | collective-permute-start | bytes 442376 | tf_op jit(solution)/shard_map/ppermute | solution.py:269
  104.1 2.1 %collective-permute-done.11 = bf16[576,128]{1,0:T(8,128)(2,1)S(1)} collective-permute-done((bf16[576,128]{1,0:T(8,128)(2,1)S(1)}, bf16[576,128]{1,0:T(8,128)(2,1)S(1)}, u32[]{:S(2)}, u32[]{:S(2)}) %collective-permute-start.11) | collective-permute-done | bytes 147488 | tf_op jit(solution)/shard_map/ppermute | solution.py:269
  107.3 3.0 %collective-permute-done.9 = bf16[576,128]{1,0:T(8,128)(2,1)S(1)} collective-permute-done((bf16[576,128]{1,0:T(8,128)(2,1)S(1)}, bf16[576,128]{1,0:T(8,128)(2,1)S(1)}, u32[]{:S(2)}, u32[]{:S(2)}) %collective-permute-start.9) | collective-permute-done | bytes 147488 | tf_op jit(solution)/shard_map/ppermute | solution.py:269
  110.4 3.7 %collective-permute-start.12 = (bf16[576,128]{1,0:T(8,128)(2,1)S(1)}, bf16[576,128]{1,0:T(8,128)(2,1)S(1)}, u32[]{:S(2)}, u32[]{:S(2)}) collective-permute-start(bf16[576,128]{1,0:T(8,128)(2,1)S(1)} %add_convert_fusion.1), channel_id=1, source_target_pairs={{0,8},{1,9},{2,10},{3,11},{4,12},{5,13},{6,14},{7,15},{8,0},{9,1},... | collective-permute-start | bytes 442376 | tf_op jit(solution)/shard_map/ppermute | solution.py:271
  114.0 15.5 %collective-permute-done.12 = bf16[576,128]{1,0:T(8,128)(2,1)S(1)} collective-permute-done((bf16[576,128]{1,0:T(8,128)(2,1)S(1)}, bf16[576,128]{1,0:T(8,128)(2,1)S(1)}, u32[]{:S(2)}, u32[]{:S(2)}) %collective-permute-start.12) | collective-permute-done | bytes 147488 | tf_op jit(solution)/shard_map/ppermute | solution.py:271
  131.8 1.8 %all-to-all-done.2.rest = bf16[8,1408,128]{2,1,0:T(8,128)(2,1)S(1)} async-done(((bf16[8,1408,128]{2,1,0:T(8,128)(2,1)}), bf16[8,1408,128]{2,1,0:T(8,128)(2,1)S(1)}, u32[]{:S(2)}, u32[]{:S(2)}) %all-to-all-start.2) | async-done | bytes 2883616 | tf_op jit(solution)/shard_map/all_to_all | solution.py:284
  133.7 1.6 %copy-done = bf16[8,1408,128]{2,1,0:T(8,128)(2,1)} copy-done((bf16[8,1408,128]{2,1,0:T(8,128)(2,1)}, bf16[8,1408,128]{2,1,0:T(8,128)(2,1)S(1)}, u32[]{:S(2)}) %copy-start) | copy-done | bytes 2883608
  135.2 4.5 %finish.1 = (bf16[256,1024]{1,0:T(8,128)(2,1)}, bf16[256,512]{1,0:T(8,128)(2,1)}, f32[512,1024]{1,0:T(8,128)}, f32[512,1024]{1,0:T(8,128)}) custom-call(bf16[8,1408,128]{2,1,0:T(8,128)(2,1)} %copy-done), custom_call_target="tpu_custom_call" | custom-call | tf_op jit(solution)/shard_map/finish/pallas_call | solution.py:227
  (41 shorter events, 7.8 us)
Async XLA Ops:
  0.6 8.6 %copy-start.9 = (bf16[256,576]{0,1:T(8,128)(2,1)S(1)}, bf16[256,576]{0,1:T(8,128)(2,1)}, u32[]{:S(2)}) copy-start(bf16[256,576]{0,1:T(8,128)(2,1)} %param.10) | copy-start | bytes 884740
  3.3 44.2 %all-to-all-start = ((bf16[8,640,128]{2,1,0:T(8,128)(2,1)}), bf16[8,640,128]{2,1,0:T(8,128)(2,1)S(1)}, u32[]{:S(2)}, u32[]{:S(2)}) async-start(bf16[8,640,128]{2,1,0:T(8,128)(2,1)} %pack.1), calls=%async_computation | async-start | bytes 2621440 | tf_op jit(solution)/shard_map/all_to_all | solution.py:280
  9.2 19.5 %collective-permute-start = (bf16[576,128]{1,0:T(8,128)(2,1)S(1)}, bf16[576,128]{1,0:T(8,128)(2,1)S(1)}, u32[]{:S(2)}, u32[]{:S(2)}) collective-permute-start(bf16[576,128]{1,0:T(8,128)(2,1)S(1)} %get-tuple-element.28), channel_id=1, source_target_pairs={{0,16},{16,0},{32,48},{48,32},{64,80},{80,64},{96,112},{112,96},{1... | collective-permute-start | bytes 442376 | tf_op jit(solution)/shard_map/ppermute | solution.py:262
  28.8 18.7 %copy-start.2 = (bf16[2,576,128]{2,1,0:T(8,128)(2,1)}, bf16[2,576,128]{2,1,0:T(8,128)(2,1)S(1)}, u32[]{:S(2)}) copy-start(bf16[2,576,128]{2,1,0:T(8,128)(2,1)S(1)} %pad_maximum_fusion.refs_0_) | copy-start | bytes 884740
  28.8 9.6 %collective-permute-start.6 = (bf16[2,576,128]{2,1,0:T(8,128)(2,1)S(1)}, bf16[2,576,128]{2,1,0:T(8,128)(2,1)S(1)}, u32[]{:S(2)}, u32[]{:S(2)}) collective-permute-start(bf16[2,576,128]{2,1,0:T(8,128)(2,1)S(1)} %pad_maximum_fusion.refs_0_), channel_id=1, source_target_pairs={{96,0},{112,16},{0,32},{16,48},{32,64},{48,80},{64,96},{80,112},{9... | collective-permute-start | bytes 884744 | tf_op jit(solution)/shard_map/ppermute | solution.py:263
  30.3 15.0 %collective-permute-start.4 = (bf16[2,576,128]{2,1,0:T(8,128)(2,1)S(1)}, bf16[2,576,128]{2,1,0:T(8,128)(2,1)S(1)}, u32[]{:S(2)}, u32[]{:S(2)}) collective-permute-start(bf16[2,576,128]{2,1,0:T(8,128)(2,1)S(1)} %pad_maximum_fusion.refs_0_), channel_id=1, source_target_pairs={{64,0},{80,16},{96,32},{112,48},{0,64},{16,80},{32,96},{48,112},{6... | collective-permute-start | bytes 884744 | tf_op jit(solution)/shard_map/ppermute | solution.py:263
  33.0 12.3 %collective-permute-start.2 = (bf16[2,576,128]{2,1,0:T(8,128)(2,1)S(1)}, bf16[2,576,128]{2,1,0:T(8,128)(2,1)S(1)}, u32[]{:S(2)}, u32[]{:S(2)}) collective-permute-start(bf16[2,576,128]{2,1,0:T(8,128)(2,1)S(1)} %pad_maximum_fusion.refs_0_), channel_id=1, source_target_pairs={{32,0},{48,16},{64,32},{80,48},{96,64},{112,80},{0,96},{16,112},{3... | collective-permute-start | bytes 884744 | tf_op jit(solution)/shard_map/ppermute | solution.py:263
  34.5 12.0 %collective-permute-start.1 = (bf16[2,576,128]{2,1,0:T(8,128)(2,1)S(1)}, bf16[2,576,128]{2,1,0:T(8,128)(2,1)S(1)}, u32[]{:S(2)}, u32[]{:S(2)}) collective-permute-start(bf16[2,576,128]{2,1,0:T(8,128)(2,1)S(1)} %pad_maximum_fusion.refs_0_), channel_id=1, source_target_pairs={{0,1},{1,0},{2,3},{3,2},{4,5},{5,4},{6,7},{7,6},{8,9},{9,8},{10,11... | collective-permute-start | bytes 884744 | tf_op jit(solution)/shard_map/ppermute | solution.py:264
  38.4 9.0 %copy-start.3 = (bf16[2,576,128]{2,1,0:T(8,128)(2,1)}, bf16[2,576,128]{2,1,0:T(8,128)(2,1)S(1)}, u32[]{:S(2)}) copy-start(bf16[2,576,128]{2,1,0:T(8,128)(2,1)S(1)} %collective-permute-done.6.refs_6_) | copy-start | bytes 884740
  38.4 8.0 %collective-permute-start.7 = (bf16[2,576,128]{2,1,0:T(8,128)(2,1)S(1)}, bf16[2,576,128]{2,1,0:T(8,128)(2,1)S(1)}, u32[]{:S(2)}, u32[]{:S(2)}) collective-permute-start(bf16[2,576,128]{2,1,0:T(8,128)(2,1)S(1)} %collective-permute-done.6.refs_6_), channel_id=1, source_target_pairs={{0,1},{1,0},{2,3},{3,2},{4,5},{5,4},{6,7},{7,6},{8,9},{9,8},{10,11... | collective-permute-start | bytes 884744 | tf_op jit(solution)/shard_map/ppermute | solution.py:264
  45.3 2.2 %copy-start.4 = (bf16[2,576,128]{2,1,0:T(8,128)(2,1)}, bf16[2,576,128]{2,1,0:T(8,128)(2,1)S(1)}, u32[]{:S(2)}) copy-start(bf16[2,576,128]{2,1,0:T(8,128)(2,1)S(1)} %collective-permute-done.4.refs_4_) | copy-start | bytes 884740
  45.3 1.6 %collective-permute-start.5 = (bf16[2,576,128]{2,1,0:T(8,128)(2,1)S(1)}, bf16[2,576,128]{2,1,0:T(8,128)(2,1)S(1)}, u32[]{:S(2)}, u32[]{:S(2)}) collective-permute-start(bf16[2,576,128]{2,1,0:T(8,128)(2,1)S(1)} %collective-permute-done.4.refs_4_), channel_id=1, source_target_pairs={{0,1},{1,0},{2,3},{3,2},{4,5},{5,4},{6,7},{7,6},{8,9},{9,8},{10,11... | collective-permute-start | bytes 884744 | tf_op jit(solution)/shard_map/ppermute | solution.py:264
  45.3 2.2 %copy-start.5 = (bf16[2,576,128]{2,1,0:T(8,128)(2,1)}, bf16[2,576,128]{2,1,0:T(8,128)(2,1)S(1)}, u32[]{:S(2)}) copy-start(bf16[2,576,128]{2,1,0:T(8,128)(2,1)S(1)} %collective-permute-done.2.refs_2_) | copy-start | bytes 884740
  45.3 2.1 %collective-permute-start.3 = (bf16[2,576,128]{2,1,0:T(8,128)(2,1)S(1)}, bf16[2,576,128]{2,1,0:T(8,128)(2,1)}, u32[]{:S(2)}, u32[]{:S(2)}) collective-permute-start(bf16[2,576,128]{2,1,0:T(8,128)(2,1)S(1)} %collective-permute-done.2.refs_2_), channel_id=1, source_target_pairs={{0,1},{1,0},{2,3},{3,2},{4,5},{5,4},{6,7},{7,6},{8,9},{9,8},{10,11... | collective-permute-start | bytes 884744 | tf_op jit(solution)/shard_map/ppermute | solution.py:264
  46.5 1.0 copy-start.7
  47.6 1.1 copy-start.1
  88.8 44.9 %all-to-all-start.2 = ((bf16[8,1408,128]{2,1,0:T(8,128)(2,1)}), bf16[8,1408,128]{2,1,0:T(8,128)(2,1)S(1)}, u32[]{:S(2)}, u32[]{:S(2)}) async-start(bf16[8,1408,128]{2,1,0:T(8,128)(2,1)} %get-tuple-element.17), calls=%async_computation.2 | async-start | bytes 5767168 | tf_op jit(solution)/shard_map/all_to_all | solution.py:284
  96.4 1.6 %collective-permute-start.8 = (bf16[576,128]{1,0:T(8,128)(2,1)}, bf16[576,128]{1,0:T(8,128)(2,1)S(1)}, u32[]{:S(2)}, u32[]{:S(2)}) collective-permute-start(bf16[576,128]{1,0:T(8,128)(2,1)} %get-tuple-element.22), channel_id=1, source_target_pairs={{0,1},{1,0},{2,3},{3,2},{4,5},{5,4},{6,7},{7,6},{8,9},{9,8},{10,11... | collective-permute-start | bytes 442376 | tf_op jit(solution)/shard_map/ppermute | solution.py:268
  99.0 7.2 %collective-permute-start.11 = (bf16[576,128]{1,0:T(8,128)(2,1)S(1)}, bf16[576,128]{1,0:T(8,128)(2,1)S(1)}, u32[]{:S(2)}, u32[]{:S(2)}) collective-permute-start(bf16[576,128]{1,0:T(8,128)(2,1)S(1)} %add_convert_fusion.2), channel_id=1, source_target_pairs={{6,0},{7,1},{0,2},{1,3},{2,4},{3,5},{4,6},{5,7},{14,8},{15,9},{8,1... | collective-permute-start | bytes 442376 | tf_op jit(solution)/shard_map/ppermute | solution.py:269
  100.5 6.7 %collective-permute-start.10 = (bf16[576,128]{1,0:T(8,128)(2,1)S(1)}, bf16[576,128]{1,0:T(8,128)(2,1)S(1)}, u32[]{:S(2)}, u32[]{:S(2)}) collective-permute-start(bf16[576,128]{1,0:T(8,128)(2,1)S(1)} %add_convert_fusion.2), channel_id=1, source_target_pairs={{2,0},{3,1},{4,2},{5,3},{6,4},{7,5},{0,6},{1,7},{10,8},{11,9},{12,... | collective-permute-start | bytes 442376 | tf_op jit(solution)/shard_map/ppermute | solution.py:269
  102.3 8.0 %collective-permute-start.9 = (bf16[576,128]{1,0:T(8,128)(2,1)S(1)}, bf16[576,128]{1,0:T(8,128)(2,1)S(1)}, u32[]{:S(2)}, u32[]{:S(2)}) collective-permute-start(bf16[576,128]{1,0:T(8,128)(2,1)S(1)} %add_convert_fusion.2), channel_id=1, source_target_pairs={{4,0},{5,1},{6,2},{7,3},{0,4},{1,5},{2,6},{3,7},{12,8},{13,9},{14,... | collective-permute-start | bytes 442376 | tf_op jit(solution)/shard_map/ppermute | solution.py:269
  110.4 19.2 %collective-permute-start.12 = (bf16[576,128]{1,0:T(8,128)(2,1)S(1)}, bf16[576,128]{1,0:T(8,128)(2,1)S(1)}, u32[]{:S(2)}, u32[]{:S(2)}) collective-permute-start(bf16[576,128]{1,0:T(8,128)(2,1)S(1)} %add_convert_fusion.1), channel_id=1, source_target_pairs={{0,8},{1,9},{2,10},{3,11},{4,12},{5,13},{6,14},{7,15},{8,0},{9,1},... | collective-permute-start | bytes 442376 | tf_op jit(solution)/shard_map/ppermute | solution.py:271
  129.6 1.5 %collective-permute-start.13 = (bf16[576,128]{1,0:T(8,128)(2,1)S(1)}, bf16[576,128]{1,0:T(8,128)(2,1)S(1)}, u32[]{:S(2)}, u32[]{:S(2)}) collective-permute-start(bf16[576,128]{1,0:T(8,128)(2,1)S(1)} %add_convert_fusion), channel_id=1, source_target_pairs={{0,1},{1,0},{2,3},{3,2},{4,5},{5,4},{6,7},{7,6},{8,9},{9,8},{10,11... | collective-permute-start | bytes 442376 | tf_op jit(solution)/shard_map/ppermute | solution.py:286
  133.7 1.6 %copy-start = (bf16[8,1408,128]{2,1,0:T(8,128)(2,1)}, bf16[8,1408,128]{2,1,0:T(8,128)(2,1)S(1)}, u32[]{:S(2)}) copy-start(bf16[8,1408,128]{2,1,0:T(8,128)(2,1)S(1)} %all-to-all-done.2.rest) | copy-start | bytes 8650756
  (2 other events, 1.7 us)

commit v3 on v2

v3 whole, which is shorter than its diff:
```python
import functools
import math

import jax
import jax.numpy as jnp
from jax import lax
from jax.experimental import pallas as pl
from jax.experimental.pallas import tpu as pltpu
from jax.sharding import PartitionSpec as P

NOPE = 128
ROPE = 64
VHEAD = 128
LATENT = 512
WIDTH = LATENT + ROPE
GROUP = 128
GROUPS = 16
TOKENS = GROUP * GROUPS
CTX = 8
HEAD = 16
MSCALE = 0.1 * math.log(40.0) + 1.0
SCALE = (NOPE + ROPE) ** (-0.5) * MSCALE * MSCALE
BLOCK = 256
BLOCKS = TOKENS // BLOCK
F32 = jnp.float32
BF16 = jnp.bfloat16
VMEM = pl.BlockSpec(memory_space=pltpu.VMEM)
SMEM = pl.BlockSpec(memory_space=pltpu.SMEM)
HBM = pl.BlockSpec(memory_space=pltpu.HBM)
BIG = pltpu.CompilerParams(vmem_limit_bytes=28 * 1024 * 1024)
PARAMS = pltpu.CompilerParams(vmem_limit_bytes=14 * 1024 * 1024)


def near(x):
    return pltpu.with_memory_space_constraint(x, pltpu.VMEM)


def far(x):
    return pltpu.with_memory_space_constraint(x, pltpu.HBM)


def nt(a, b):
    return lax.dot_general(a, b, (((1,), (1,)), ((), ())), preferred_element_type=F32)


def nn(a, b):
    return jnp.dot(a, b, preferred_element_type=F32)


def pack_kernel(q, r, g, send, rope, sems):
    first = pltpu.make_async_copy(r, rope, sems.at[0])
    first.start()
    copies = []
    for i in range(CTX):
        cols = slice(i * 128, (i + 1) * 128)
        copies.append(pltpu.make_async_copy(q.at[:, cols], send.at[i, :256, :], sems.at[1 + 2 * i]))
        copies.append(pltpu.make_async_copy(g.at[:, cols], send.at[i, 256:512, :], sems.at[2 + 2 * i]))
    for copy in copies:
        copy.start()
    first.wait()
    for i in range(CTX):
        part = rope[:, i * ROPE:(i + 1) * ROPE]
        send[i, 512:, :] = jnp.concatenate([part[:128], part[128:]], axis=1)
    for copy in copies:
        copy.wait()


def pack(q, r, g):
    return pl.pallas_call(
        pack_kernel,
        out_shape=jax.ShapeDtypeStruct((CTX, 640, 128), BF16),
        in_specs=[HBM, HBM, HBM],
        out_specs=VMEM,
        scratch_shapes=[pltpu.VMEM((256, CTX * ROPE), BF16), pltpu.SemaphoreType.DMA((17,))],
        compiler_params=PARAMS,
        name="pack",
    )(far(q), far(r), far(g))


def head_kernel(order, place, recv, *refs):
    latents, (uk_all, uv_all, keys, rest) = refs[:6], refs[6:10]
    uk, uv, val, qf, go, kf, kt, vf, gk, gv, gq, grads_w, grads_q, sems = refs[10:]
    column = pl.ds(pl.multiple_of(place[0] * NOPE, NOPE), NOPE)
    uk_copy = pltpu.make_async_copy(uk_all.at[:, column], uk, sems.at[0])
    uv_copy = pltpu.make_async_copy(uv_all.at[:, column], uv, sems.at[1])
    uk_copy.start()
    uv_copy.start()
    me, core = place[0], place[1]
    y, z = me // 2, lax.rem(me, 2)

    def at(s):
        return pl.ds(pl.multiple_of(order[s] * GROUP, GROUP), GROUP)

    for rc in range(2):
        pair, trio, trio_z = latents[rc::2]
        pieces = [(0, 0, pair, 0), (0, 1, pair, 1)]
        for t, dy in enumerate((3, 1, 2)):
            pieces += [(dy, 0, trio, t), (dy, 1, trio_z, t)]
        for dy, rz, src, t in pieces:
            c = lax.rem(y + dy, 4) * 2 + lax.rem(z + rz, 2)
            cols = at(c * 2 + lax.rem(core + rc, 2))
            val[:, cols] = src[t, :LATENT, :]
            kt[NOPE:, cols] = src[t, LATENT:, :]
    for s in range(GROUPS):
        c, b = s // 2, s % 2
        rows = at(s)
        qf[rows, :NOPE] = recv[c, b * 128:(b + 1) * 128, :]
        go[rows, :] = recv[c, 256 + b * 128:256 + (b + 1) * 128, :]
        qf[rows, NOPE:] = recv[c, 512:640, b * ROPE:(b + 1) * ROPE]

    uk_copy.wait()
    uv_copy.wait()
    ukt = jnp.transpose(uk[...].astype(F32)).astype(BF16)
    uvt = jnp.transpose(uv[...].astype(F32)).astype(BF16)
    for p in range(BLOCKS):
        rows = slice(p * BLOCK, (p + 1) * BLOCK)
        latent = val[:, rows]
        k_t = nn(ukt, latent)
        kt[:NOPE, rows] = k_t.astype(BF16)
        kf[rows, :NOPE] = jnp.transpose(k_t).astype(BF16)
        kf[rows, NOPE:] = jnp.transpose(kt[NOPE:, rows].astype(F32)).astype(BF16)
        vf[rows, :] = jnp.transpose(nn(uvt, latent)).astype(BF16)

    factor = SCALE * math.log2(math.e)
    key_at = lax.broadcasted_iota(jnp.int32, (BLOCK, BLOCK), 0)
    query_at = lax.broadcasted_iota(jnp.int32, (BLOCK, BLOCK), 1)
    seen = key_at <= query_at
    def products(i):
        mine = slice(i * BLOCK, (i + 1) * BLOCK)
        scores, grads = [], []
        for j in range(i + 1):
            rows = slice(j * BLOCK, (j + 1) * BLOCK)
            s = nt(kf[rows, :], qf[mine, :]) * factor
            scores.append(jnp.where(seen, s, -jnp.inf) if j == i else s)
            grads.append(nt(vf[rows, :], go[mine, :]))
        return scores, grads

    ahead = products(0)
    for i in range(BLOCKS):
        mine = slice(i * BLOCK, (i + 1) * BLOCK)
        q_i, g_i = qf[mine, :], go[mine, :]
        scores, grads = ahead
        if i + 1 < BLOCKS:
            ahead = products(i + 1)
        top = functools.reduce(jnp.maximum, [jnp.max(s, axis=0, keepdims=True) for s in scores])
        expo = [jnp.exp2(s - top) for s in scores]
        total = functools.reduce(jnp.add, [jnp.sum(e, axis=0, keepdims=True) for e in expo])
        inverse = 1.0 / total
        delta = functools.reduce(
            jnp.add, [jnp.sum(e * d, axis=0, keepdims=True) for e, d in zip(expo, grads)]
        ) * inverse
        acc = None
        for j in range(i + 1):
            rows = slice(j * BLOCK, (j + 1) * BLOCK)
            probs = expo[j] * inverse
            ds = (probs * (grads[j] - delta)).astype(BF16)
            part = nn(kt[:, rows], ds)
            acc = part if acc is None else acc + part
            to_k = nn(ds, q_i)
            to_v = nn(probs.astype(BF16), g_i)
            if j == i:
                gk[rows, :] = to_k
                gv[rows, :] = to_v
            else:
                gk[rows, :] += to_k
                gv[rows, :] += to_v
        gq[mine, :] = jnp.transpose(acc) * SCALE

    gkb = (gk[...] * SCALE).astype(BF16)
    gvb = gv[...].astype(BF16)
    guk = nn(val[...], gkb[:, :NOPE]).astype(BF16)
    guv = nn(val[...], gvb).astype(BF16)
    kf[...] = gkb
    vf[...] = gvb
    grads_w[:LATENT, :] = guk
    grads_w[LATENT:, :] = guv
    copies = [
        pltpu.make_async_copy(grads_w, rest.at[c, 384:, :], sems.at[2 + c]) for c in range(CTX)
    ]
    for c in range(CTX):
        copies[c].start()
        lo, hi = at(2 * c), at(2 * c + 1)
        first, second = gq[lo, :], gq[hi, :]
        grads_q[c, :128, :] = first[:, :NOPE].astype(BF16)
        grads_q[c, 128:256, :] = second[:, :NOPE].astype(BF16)
        grads_q[c, 256:384, :] = jnp.concatenate(
            [first[:, NOPE:], second[:, NOPE:]], axis=1
        ).astype(BF16)
        copies.append(
            pltpu.make_async_copy(grads_q.at[c], rest.at[c, :384, :], sems.at[2 + CTX + c])
        )
        copies[-1].start()
    for c in range(CTX):
        lo, hi = at(2 * c), at(2 * c + 1)
        keys[c, :128, :] = kf[lo, :NOPE]
        keys[c, 128:256, :] = kf[hi, :NOPE]
        keys[c, 256:384, :] = vf[lo, :]
        keys[c, 384:512, :] = vf[hi, :]
        keys[c, 512:, :] = jnp.concatenate([kf[lo, NOPE:], kf[hi, NOPE:]], axis=1)
    for copy in copies:
        copy.wait()


def head_call(order, place, recv, latents, uk, uv):
    return pl.pallas_call(
        head_kernel,
        out_shape=(
            pltpu.VMEM((CTX, 640, 128), BF16),
            pltpu.HBM((CTX, 1408, 128), BF16),
        ),
        in_specs=[SMEM, SMEM] + [VMEM] * 7 + [HBM, HBM],
        out_specs=(VMEM, HBM),
        scratch_shapes=[
            pltpu.VMEM((LATENT, NOPE), BF16),
            pltpu.VMEM((LATENT, VHEAD), BF16),
            pltpu.VMEM((LATENT, TOKENS), BF16),
            pltpu.VMEM((TOKENS, NOPE + ROPE), BF16),
            pltpu.VMEM((TOKENS, VHEAD), BF16),
            pltpu.VMEM((TOKENS, NOPE + ROPE), BF16),
            pltpu.VMEM((NOPE + ROPE, TOKENS), BF16),
            pltpu.VMEM((TOKENS, VHEAD), BF16),
            pltpu.VMEM((TOKENS, NOPE + ROPE), F32),
            pltpu.VMEM((TOKENS, VHEAD), F32),
            pltpu.VMEM((TOKENS, NOPE + ROPE), F32),
            pltpu.VMEM((2 * LATENT, 128), BF16),
            pltpu.VMEM((CTX, 384, 128), BF16),
            pltpu.SemaphoreType.DMA((2 + 2 * CTX,)),
        ],
        compiler_params=BIG,
        name="head",
    )(order, place, near(recv), *[near(x) for x in latents], far(uk), far(uv))


def post_kernel(place, back_all, uk_all, uv_all, own, away, back, uk, uv, sems):
    copies = [
        pltpu.make_async_copy(src, dst, sems.at[k])
        for k, (src, dst) in enumerate(((back_all, back), (uk_all, uk), (uv_all, uv)))
    ]
    for copy in copies:
        copy.start()
    for copy in copies:
        copy.wait()
    acc = rope = None
    for i in range(CTX):
        cols = slice(i * 128, (i + 1) * 128)
        part = nt(uk[:, cols], back[i, :256, :]) + nt(uv[:, cols], back[i, 256:512, :])
        tail = back[i, 512:, :].astype(F32)
        acc = part if acc is None else acc + part
        rope = tail if rope is None else rope + tail
    turned = jnp.transpose(rope)
    low = place[1] == 0
    own[:LATENT, :] = jnp.where(low, acc[:, :128], acc[:, 128:])
    own[LATENT:, :] = jnp.where(low, turned[:ROPE], turned[ROPE:])
    away[:LATENT, :] = jnp.where(low, acc[:, 128:], acc[:, :128]).astype(BF16)
    away[LATENT:, :] = jnp.where(low, turned[ROPE:], turned[:ROPE]).astype(BF16)


def post(place, back, uk, uv):
    return pl.pallas_call(
        post_kernel,
        out_shape=(
            pltpu.VMEM((WIDTH, 128), F32),
            pltpu.VMEM((WIDTH, 128), BF16),
        ),
        in_specs=[SMEM, HBM, HBM, HBM],
        out_specs=(VMEM, VMEM),
        scratch_shapes=[
            pltpu.VMEM((CTX, 640, 128), BF16),
            pltpu.VMEM((LATENT, 1024), BF16),
            pltpu.VMEM((LATENT, 1024), BF16),
            pltpu.SemaphoreType.DMA((3,)),
        ],
        compiler_params=PARAMS,
        name="post",
    )(place, far(back), far(uk), far(uv))


def finish_kernel(rest, gqn, gqr, guk, guv, qn, qr, uk, uv, sems):
    copies = []
    for t in range(CTX):
        cols = slice(128 * t, 128 * (t + 1))
        uk[:, cols] = rest[t, 384:896, :].astype(F32)
        uv[:, cols] = rest[t, 896:, :].astype(F32)
        qn[:, cols] = rest[t, :256, :]
        pair = rest[t, 256:384, :]
        qr[:128, ROPE * t:ROPE * (t + 1)] = pair[:, :ROPE]
        qr[128:, ROPE * t:ROPE * (t + 1)] = pair[:, ROPE:]
        if t % 2 == 1:
            wide = slice(128 * (t - 1), 128 * (t + 1))
            for k, (src, dst) in enumerate(((uk, guk), (uv, guv))):
                copies.append(
                    pltpu.make_async_copy(src.at[:, wide], dst.at[:, wide], sems.at[t // 2 * 2 + k])
                )
                copies[-1].start()
    for k, (src, dst) in enumerate(((qn, gqn), (qr, gqr))):
        copies.append(pltpu.make_async_copy(src, dst, sems.at[8 + k]))
        copies[-1].start()
    for copy in copies:
        copy.wait()


def finish(rest):
    shapes = (((256, 1024), BF16), ((256, 512), BF16), ((LATENT, 1024), F32), ((LATENT, 1024), F32))
    return pl.pallas_call(
        finish_kernel,
        out_shape=tuple(jax.ShapeDtypeStruct(*shape) for shape in shapes),
        in_specs=[VMEM],
        out_specs=(HBM,) * 4,
        scratch_shapes=[pltpu.VMEM(*shape) for shape in shapes] + [pltpu.SemaphoreType.DMA((10,))],
        compiler_params=PARAMS,
        name="finish",
    )(near(rest))


CORE_SWAP = [(i, i ^ 1) for i in range(HEAD)]
ZLO_SWAP = [(i, i ^ 1) for i in range(CTX)]
ZHI_SWAP = [(i, i ^ 8) for i in range(HEAD)]


def from_y(step):
    return [(((c // 2 + step) % 4) * 2 + c % 2, c) for c in range(CTX)]


def from_x(step):
    return [((h & 8) + ((h // 2 + step) % 4) * 2 + h % 2, h) for h in range(HEAD)]


def gather_latent(half, other, trio):
    found = (jnp.stack([half, other]), trio, lax.ppermute(trio, "ctx", ZLO_SWAP))
    return [part for f in found for part in (f, lax.ppermute(f, "head", CORE_SWAP))]


def sum_heads(own, away):
    pair = (own + lax.ppermute(away, "head", CORE_SWAP).astype(F32)).astype(BF16)
    one, two, three = (lax.ppermute(pair, "head", from_x(d)).astype(F32) for d in (1, 2, 3))
    quad = ((pair.astype(F32) + two) + (one + three)).astype(BF16)
    far = lax.ppermute(quad, "head", ZHI_SWAP)
    return (quad.astype(F32) + far.astype(F32)).astype(BF16)


def on_device(q_nope, q_rope, grad_out, kv_latent, w_uk, w_uv, group_order):
    core = lax.axis_index("head") % 2
    place = jnp.stack([lax.axis_index("ctx"), core]).astype(jnp.int32)
    half = lax.dynamic_slice_in_dim(kv_latent.T, core * GROUP, GROUP, 1)
    other = lax.ppermute(half, "ctx", ZLO_SWAP)
    trio = jnp.stack([lax.ppermute(half, "ctx", from_y(d)) for d in (3, 1, 2)])
    packed = pack(q_nope, q_rope, grad_out)
    latents = gather_latent(half, other, trio)
    recv = lax.all_to_all(packed, "ctx", 0, 0, tiled=True)
    keys, rest = head_call(group_order, place, recv, latents, w_uk, w_uv)
    keys = lax.all_to_all(keys, "ctx", 0, 0, tiled=True)
    keys, rest = lax.optimization_barrier((keys, rest))
    rest = lax.all_to_all(rest, "ctx", 0, 0, tiled=True)
    total = sum_heads(*post(place, keys, w_uk, w_uv))
    peer = lax.ppermute(total, "head", CORE_SWAP)
    low = core == 0
    grad_kv = jnp.concatenate(
        [jnp.where(low, total, peer), jnp.where(low, peer, total)], axis=1
    ).T
    gqn, gqr, guk, guv = finish(rest)
    return gqn, gqr, grad_kv, guk, guv


def solution(mesh):
    in_specs = (
        P("ctx", "head"),
        P("ctx", "head"),
        P("ctx", "head"),
        P("ctx", None),
        P(None, "head"),
        P(None, "head"),
        P(),
    )
    out_specs = (
        P("ctx", "head"),
        P("ctx", "head"),
        P("ctx", None),
        P(None, "head"),
        P(None, "head"),
    )
    return jax.shard_map(
        on_device, mesh=mesh, in_specs=in_specs, out_specs=out_specs, check_vma=False
    )
```

time: 140 us -> 130 us (0.929)
  Pallas kernels: 28.2 us -> 24.1 us
  local copies, waits for them, and re-layouts: 2.81 us -> 0.96 us
  starting transfers between devices: 26.7 us -> 24.9 us
  other arithmetic: 2.56 us -> 1.09 us
    pallas_call x3, Pallas kernels: 25.6 us -> 21.6 us  [the longest x1 15.3 us: head_call(): pl.pallas_call(head_kernel, out_shape=(pltpu.VMEM((CTX, 640, 128), BF16),...]
    unnamed x20 -> x2, local copies, waits for them, and re-layouts: 2.78 us -> 0.01 us
    ppermute x4 -> x5, waiting for transfers between devices: 28.3 us -> 26 us  [the longest x1 24 us: gather_latent(): lax.ppermute(trio, 'ctx', ZLO_SWAP)]
    ppermute x4 -> x5, starting transfers between devices: 7.75 us -> 7.48 us  [the longest x3 5.37 us: on_device(): trio = jnp.stack([lax.ppermute(half, 'ctx', from_y(d)) for d in (3, 1, 2)])]
  transfers between devices with their start and end apart: 16 -> 16, of which waited for: 12 -> 11; matrix products, arithmetic and copies ran while one was open for 2% -> 1% of each run, Pallas kernels for 3% -> 5%
where the time goes in v3:
time: 130 us; the launch traced here: 129 us
  waiting for transfers between devices  54.6 us (42%)
  starting transfers between devices  24.9 us (19%)
  Pallas kernels  24.1 us (19%)
  blocking collectives  22.6 us (17%)
    ppermute x1, waiting for transfers between devices, gather_latent(): lax.ppermute(trio, 'ctx', ZLO_SWAP)  24 us
    all_to_all x1, blocking collectives, on_device(): keys = lax.all_to_all(keys, 'ctx', 0, 0, tiled=True)  22.6 us
    ppermute x1, waiting for transfers between devices, sum_heads(): far = lax.ppermute(quad, 'head', ZHI_SWAP)  16.4 us
    pallas_call x1, Pallas kernels, head_call(): pl.pallas_call(head_kernel, out_shape=(pltpu.VMEM((CTX, 640, 128), BF16),...  15.3 us
    ppermute x3, waiting for transfers between devices, sum_heads(): lax.ppermute(pair, 'head', from_x(d)).astype(F32)  6.2 us
    ppermute x3, starting transfers between devices, on_device(): trio = jnp.stack([lax.ppermute(half, 'ctx', from_y(d)) for d in (3, 1, 2)])  5.37 us
    ppermute x3, starting transfers between devices, sum_heads(): lax.ppermute(pair, 'head', from_x(d)).astype(F32)  5.12 us
    all_to_all x1, starting transfers between devices, on_device(): recv = lax.all_to_all(packed, 'ctx', 0, 0, tiled=True)  4.53 us
  transfers between devices with their start and end apart: 16, of which 11 were waited for; matrix products, arithmetic and copies ran while one was open for 1% of the time, Pallas kernels for 5%

profile of v3, /device:TPU:0, one launch (start us, length us, event | category | flops | bytes accessed | tf_op | source)
XLA Modules:
  0.0 129.2 jit_solution(7997219332046922383)
XLA Ops:
  1.6 3.2 %collective-permute-start.3 = (bf16[576,128]{1,0:T(8,128)(2,1)S(1)}, bf16[576,128]{1,0:T(8,128)(2,1)S(1)}, u32[]{:S(2)}, u32[]{:S(2)}) collective-permute-start(bf16[576,128]{1,0:T(8,128)(2,1)S(1)} %get-tuple-element.28), channel_id=1, source_target_pairs={{32,0},{48,16},{64,32},{80,48},{96,64},{112,80},{0,96},{16,112},{3... | collective-permute-start | bytes 442376 | tf_op jit(solution)/shard_map/ppermute | solution.py:346
  4.8 2.2 %collective-permute-start.4 = (bf16[576,128]{1,0:T(8,128)(2,1)S(1)}, bf16[576,128]{1,0:T(8,128)(2,1)S(1)}, u32[]{:S(2)}, u32[]{:S(2)}) collective-permute-start(bf16[576,128]{1,0:T(8,128)(2,1)S(1)} %get-tuple-element.28), channel_id=1, source_target_pairs={{64,0},{80,16},{96,32},{112,48},{0,64},{16,80},{32,96},{48,112},{6... | collective-permute-start | bytes 442376 | tf_op jit(solution)/shard_map/ppermute | solution.py:346
  7.0 2.5 %pack.1 = bf16[8,640,128]{2,1,0:T(8,128)(2,1)} custom-call(bf16[256,1024]{1,0:T(8,128)(2,1)} %q.1, bf16[256,512]{1,0:T(8,128)(2,1)} %r.1, bf16[256,1024]{1,0:T(8,128)(2,1)} %g.1), custom_call_target="tpu_custom_call" | custom-call | tf_op jit(solution)/shard_map/pack/pallas_call | solution.py:69
  9.5 4.5 %all-to-all-start = ((bf16[8,640,128]{2,1,0:T(8,128)(2,1)}), bf16[8,640,128]{2,1,0:T(8,128)(2,1)S(1)}, u32[]{:S(2)}, u32[]{:S(2)}) async-start(bf16[8,640,128]{2,1,0:T(8,128)(2,1)} %pack.1), calls=%async_computation | async-start | bytes 2621440 | tf_op jit(solution)/shard_map/all_to_all | solution.py:349
  14.5 2.0 %collective-permute-start.6 = (bf16[3,576,128]{2,1,0:T(8,128)(2,1)S(1)}, bf16[3,576,128]{2,1,0:T(8,128)(2,1)S(1)}, u32[]{:S(2)}, u32[]{:S(2)}) collective-permute-start(bf16[3,576,128]{2,1,0:T(8,128)(2,1)S(1)} %pad_maximum_fusion.refs_2_), channel_id=1, source_target_pairs={{0,16},{16,0},{32,48},{48,32},{64,80},{80,64},{96,112},{112,96},{1... | collective-permute-start | bytes 1327112 | tf_op jit(solution)/shard_map/ppermute | solution.py:329
  16.6 24.0 %collective-permute-done.6.refs_4_ = bf16[3,576,128]{2,1,0:T(8,128)(2,1)S(1)} collective-permute-done((bf16[3,576,128]{2,1,0:T(8,128)(2,1)S(1)}, bf16[3,576,128]{2,1,0:T(8,128)(2,1)S(1)}, u32[]{:S(2)}, u32[]{:S(2)}) %collective-permute-start.6) | collective-permute-done | bytes 442400 | tf_op jit(solution)/shard_map/ppermute | solution.py:329
  40.6 1.6 %collective-permute-done = bf16[576,128]{1,0:T(8,128)(2,1)S(1)} collective-permute-done((bf16[576,128]{1,0:T(8,128)(2,1)S(1)}, bf16[576,128]{1,0:T(8,128)(2,1)S(1)}, u32[]{:S(2)}, u32[]{:S(2)}) %collective-permute-start) | collective-permute-done | bytes 147488 | tf_op jit(solution)/shard_map/ppermute | solution.py:345
  42.6 1.6 %collective-permute-done.1.refs_1_ = bf16[2,576,128]{2,1,0:T(8,128)(2,1)} collective-permute-done((bf16[2,576,128]{2,1,0:T(8,128)(2,1)S(1)}, bf16[2,576,128]{2,1,0:T(8,128)(2,1)}, u32[]{:S(2)}, u32[]{:S(2)}) %collective-permute-start.1) | collective-permute-done | bytes 294944 | tf_op jit(solution)/shard_map/ppermute | solution.py:330
  44.2 15.3 %head.1 = (bf16[8,640,128]{2,1,0:T(8,128)(2,1)S(1)}, bf16[8,1408,128]{2,1,0:T(8,128)(2,1)}) custom-call(s32[16]{0:T(128)S(1)} %copy-done, s32[2]{0:T(128)S(1)} %pad_add_fusion.place, bf16[8,640,128]{2,1,0:T(8,128)(2,1)S(1)} %all-to-all-done.recv, bf16[2,576,128]{2,1,0:T(8,128)(2,1)S(1)} %pad_maximum_fusion.1.refs_0_, ...), custom_call_target="tpu_custom_call" | custom-call | tf_op jit(solution)/shard_map/head/pallas_call | solution.py:205
  59.6 22.6 %all_to_all.15.back_all = bf16[8,640,128]{2,1,0:T(8,128)(2,1)} all-to-all(bf16[8,640,128]{2,1,0:T(8,128)(2,1)S(1)} %get-tuple-element.15), channel_id=1, replica_groups=mesh['ctx'=8,'head'=16] {'ctx'}, dimensions={0} | all-to-all | bytes 2621440 | tf_op jit(solution)/shard_map/all_to_all | solution.py:351
  82.2 3.6 %all-to-all-start.2 = ((bf16[8,1408,128]{2,1,0:T(8,128)(2,1)}), bf16[8,1408,128]{2,1,0:T(8,128)(2,1)S(1)}, u32[]{:S(2)}, u32[]{:S(2)}) async-start(bf16[8,1408,128]{2,1,0:T(8,128)(2,1)} %get-tuple-element.17), calls=%async_computation.2 | async-start | bytes 5767168 | tf_op jit(solution)/shard_map/all_to_all | solution.py:353
  85.9 3.7 %post.1 = (f32[576,128]{1,0:T(8,128)S(1)}, bf16[576,128]{1,0:T(8,128)(2,1)S(1)}) custom-call(s32[2]{0:T(128)S(1)} %pad_add_fusion.place, bf16[8,640,128]{2,1,0:T(8,128)(2,1)} %all_to_all.15.back_all, bf16[512,1024]{1,0:T(8,128)(2,1)} %uk_all.1, bf16[512,1024]{1,0:T(8,128)(2,1)} %uv_all.1), custom_call_target="tpu_custom_call" | custom-call | tf_op jit(solution)/shard_map/post/pallas_call | solution.py:259
  89.7 1.4 %collective-permute-done.8 = bf16[576,128]{1,0:T(8,128)(2,1)S(1)} collective-permute-done((bf16[576,128]{1,0:T(8,128)(2,1)S(1)}, bf16[576,128]{1,0:T(8,128)(2,1)S(1)}, u32[]{:S(2)}, u32[]{:S(2)}) %collective-permute-start.8) | collective-permute-done | bytes 147488 | tf_op jit(solution)/shard_map/ppermute | solution.py:334
  91.1 1.6 %collective-permute-start.11 = (bf16[576,128]{1,0:T(8,128)(2,1)S(1)}, bf16[576,128]{1,0:T(8,128)(2,1)S(1)}, u32[]{:S(2)}, u32[]{:S(2)}) collective-permute-start(bf16[576,128]{1,0:T(8,128)(2,1)S(1)} %add_convert_fusion.2), channel_id=1, source_target_pairs={{6,0},{7,1},{0,2},{1,3},{2,4},{3,5},{4,6},{5,7},{14,8},{15,9},{8,1... | collective-permute-start | bytes 442376 | tf_op jit(solution)/shard_map/ppermute | solution.py:335
  92.7 1.7 %collective-permute-start.10 = (bf16[576,128]{1,0:T(8,128)(2,1)S(1)}, bf16[576,128]{1,0:T(8,128)(2,1)S(1)}, u32[]{:S(2)}, u32[]{:S(2)}) collective-permute-start(bf16[576,128]{1,0:T(8,128)(2,1)S(1)} %add_convert_fusion.2), channel_id=1, source_target_pairs={{2,0},{3,1},{4,2},{5,3},{6,4},{7,5},{0,6},{1,7},{10,8},{11,9},{12,... | collective-permute-start | bytes 442376 | tf_op jit(solution)/shard_map/ppermute | solution.py:335
  94.4 1.8 %collective-permute-start.9 = (bf16[576,128]{1,0:T(8,128)(2,1)S(1)}, bf16[576,128]{1,0:T(8,128)(2,1)S(1)}, u32[]{:S(2)}, u32[]{:S(2)}) collective-permute-start(bf16[576,128]{1,0:T(8,128)(2,1)S(1)} %add_convert_fusion.2), channel_id=1, source_target_pairs={{4,0},{5,1},{6,2},{7,3},{0,4},{1,5},{2,6},{3,7},{12,8},{13,9},{14,... | collective-permute-start | bytes 442376 | tf_op jit(solution)/shard_map/ppermute | solution.py:335
  96.2 2.1 %collective-permute-done.11 = bf16[576,128]{1,0:T(8,128)(2,1)S(1)} collective-permute-done((bf16[576,128]{1,0:T(8,128)(2,1)S(1)}, bf16[576,128]{1,0:T(8,128)(2,1)S(1)}, u32[]{:S(2)}, u32[]{:S(2)}) %collective-permute-start.11) | collective-permute-done | bytes 147488 | tf_op jit(solution)/shard_map/ppermute | solution.py:335
  98.3 2.5 %collective-permute-done.10 = bf16[576,128]{1,0:T(8,128)(2,1)S(1)} collective-permute-done((bf16[576,128]{1,0:T(8,128)(2,1)S(1)}, bf16[576,128]{1,0:T(8,128)(2,1)S(1)}, u32[]{:S(2)}, u32[]{:S(2)}) %collective-permute-start.10) | collective-permute-done | bytes 147488 | tf_op jit(solution)/shard_map/ppermute | solution.py:335
  100.7 1.7 %collective-permute-done.9 = bf16[576,128]{1,0:T(8,128)(2,1)S(1)} collective-permute-done((bf16[576,128]{1,0:T(8,128)(2,1)S(1)}, bf16[576,128]{1,0:T(8,128)(2,1)S(1)}, u32[]{:S(2)}, u32[]{:S(2)}) %collective-permute-start.9) | collective-permute-done | bytes 147488 | tf_op jit(solution)/shard_map/ppermute | solution.py:335
  102.5 3.7 %collective-permute-start.12 = (bf16[576,128]{1,0:T(8,128)(2,1)S(1)}, bf16[576,128]{1,0:T(8,128)(2,1)S(1)}, u32[]{:S(2)}, u32[]{:S(2)}) collective-permute-start(bf16[576,128]{1,0:T(8,128)(2,1)S(1)} %add_convert_fusion.1), channel_id=1, source_target_pairs={{0,8},{1,9},{2,10},{3,11},{4,12},{5,13},{6,14},{7,15},{8,0},{9,1},... | collective-permute-start | bytes 442376 | tf_op jit(solution)/shard_map/ppermute | solution.py:337
  106.2 16.4 %collective-permute-done.12 = bf16[576,128]{1,0:T(8,128)(2,1)S(1)} collective-permute-done((bf16[576,128]{1,0:T(8,128)(2,1)S(1)}, bf16[576,128]{1,0:T(8,128)(2,1)S(1)}, u32[]{:S(2)}, u32[]{:S(2)}) %collective-permute-start.12) | collective-permute-done | bytes 147488 | tf_op jit(solution)/shard_map/ppermute | solution.py:337
  122.7 1.4 %collective-permute-done.13 = bf16[576,128]{1,0:T(8,128)(2,1)S(1)} collective-permute-done((bf16[576,128]{1,0:T(8,128)(2,1)S(1)}, bf16[576,128]{1,0:T(8,128)(2,1)S(1)}, u32[]{:S(2)}, u32[]{:S(2)}) %collective-permute-start.13) | collective-permute-done | bytes 147488 | tf_op jit(solution)/shard_map/ppermute | solution.py:355
  124.9 1.6 %all-to-all-done.2.rest = bf16[8,1408,128]{2,1,0:T(8,128)(2,1)S(1)} async-done(((bf16[8,1408,128]{2,1,0:T(8,128)(2,1)}), bf16[8,1408,128]{2,1,0:T(8,128)(2,1)S(1)}, u32[]{:S(2)}, u32[]{:S(2)}) %all-to-all-start.2) | async-done | bytes 2883616 | tf_op jit(solution)/shard_map/all_to_all | solution.py:353
  126.5 2.5 %finish.1 = (bf16[256,1024]{1,0:T(8,128)(2,1)}, bf16[256,512]{1,0:T(8,128)(2,1)}, f32[512,1024]{1,0:T(8,128)}, f32[512,1024]{1,0:T(8,128)}) custom-call(bf16[8,1408,128]{2,1,0:T(8,128)(2,1)S(1)} %all-to-all-done.2.rest), custom_call_target="tpu_custom_call" | custom-call | tf_op jit(solution)/shard_map/finish/pallas_call | solution.py:304
  (24 shorter events, 3.0 us)
Async XLA Ops:
  1.6 12.4 %collective-permute-start.3 = (bf16[576,128]{1,0:T(8,128)(2,1)S(1)}, bf16[576,128]{1,0:T(8,128)(2,1)S(1)}, u32[]{:S(2)}, u32[]{:S(2)}) collective-permute-start(bf16[576,128]{1,0:T(8,128)(2,1)S(1)} %get-tuple-element.28), channel_id=1, source_target_pairs={{32,0},{48,16},{64,32},{80,48},{96,64},{112,80},{0,96},{16,112},{3... | collective-permute-start | bytes 442376 | tf_op jit(solution)/shard_map/ppermute | solution.py:346
  4.8 9.7 %collective-permute-start.2 = (bf16[576,128]{1,0:T(8,128)(2,1)S(1)}, bf16[576,128]{1,0:T(8,128)(2,1)S(1)}, u32[]{:S(2)}, u32[]{:S(2)}) collective-permute-start(bf16[576,128]{1,0:T(8,128)(2,1)S(1)} %get-tuple-element.28), channel_id=1, source_target_pairs={{96,0},{112,16},{0,32},{16,48},{32,64},{48,80},{64,96},{80,112},{9... | collective-permute-start | bytes 442376 | tf_op jit(solution)/shard_map/ppermute | solution.py:346
  4.8 9.7 %collective-permute-start.4 = (bf16[576,128]{1,0:T(8,128)(2,1)S(1)}, bf16[576,128]{1,0:T(8,128)(2,1)S(1)}, u32[]{:S(2)}, u32[]{:S(2)}) collective-permute-start(bf16[576,128]{1,0:T(8,128)(2,1)S(1)} %get-tuple-element.28), channel_id=1, source_target_pairs={{64,0},{80,16},{96,32},{112,48},{0,64},{16,80},{32,96},{48,112},{6... | collective-permute-start | bytes 442376 | tf_op jit(solution)/shard_map/ppermute | solution.py:346
  9.5 34.8 %copy-start = (s32[16]{0:T(128)S(1)}, s32[16]{0:T(128)}, u32[]{:S(2)}) copy-start(s32[16]{0:T(128)} %order.1) | copy-start | bytes 196
  9.5 34.7 %all-to-all-start = ((bf16[8,640,128]{2,1,0:T(8,128)(2,1)}), bf16[8,640,128]{2,1,0:T(8,128)(2,1)S(1)}, u32[]{:S(2)}, u32[]{:S(2)}) async-start(bf16[8,640,128]{2,1,0:T(8,128)(2,1)} %pack.1), calls=%async_computation | async-start | bytes 2621440 | tf_op jit(solution)/shard_map/all_to_all | solution.py:349
  14.5 26.1 %collective-permute-start.6 = (bf16[3,576,128]{2,1,0:T(8,128)(2,1)S(1)}, bf16[3,576,128]{2,1,0:T(8,128)(2,1)S(1)}, u32[]{:S(2)}, u32[]{:S(2)}) collective-permute-start(bf16[3,576,128]{2,1,0:T(8,128)(2,1)S(1)} %pad_maximum_fusion.refs_2_), channel_id=1, source_target_pairs={{0,16},{16,0},{32,48},{48,32},{64,80},{80,64},{96,112},{112,96},{1... | collective-permute-start | bytes 1327112 | tf_op jit(solution)/shard_map/ppermute | solution.py:329
  16.5 25.7 %collective-permute-start = (bf16[576,128]{1,0:T(8,128)(2,1)S(1)}, bf16[576,128]{1,0:T(8,128)(2,1)S(1)}, u32[]{:S(2)}, u32[]{:S(2)}) collective-permute-start(bf16[576,128]{1,0:T(8,128)(2,1)S(1)} %get-tuple-element.28), channel_id=1, source_target_pairs={{0,16},{16,0},{32,48},{48,32},{64,80},{80,64},{96,112},{112,96},{1... | collective-permute-start | bytes 442376 | tf_op jit(solution)/shard_map/ppermute | solution.py:345
  16.6 27.6 %collective-permute-start.5 = (bf16[3,576,128]{2,1,0:T(8,128)(2,1)S(1)}, bf16[3,576,128]{2,1,0:T(8,128)(2,1)S(1)}, u32[]{:S(2)}, u32[]{:S(2)}) collective-permute-start(bf16[3,576,128]{2,1,0:T(8,128)(2,1)S(1)} %pad_maximum_fusion.refs_2_), channel_id=1, source_target_pairs={{0,1},{1,0},{2,3},{3,2},{4,5},{5,4},{6,7},{7,6},{8,9},{9,8},{10,11... | collective-permute-start | bytes 1327112 | tf_op jit(solution)/shard_map/ppermute | solution.py:330
  40.6 3.6 %collective-permute-start.7 = (bf16[3,576,128]{2,1,0:T(8,128)(2,1)S(1)}, bf16[3,576,128]{2,1,0:T(8,128)(2,1)S(1)}, u32[]{:S(2)}, u32[]{:S(2)}) collective-permute-start(bf16[3,576,128]{2,1,0:T(8,128)(2,1)S(1)} %collective-permute-done.6.refs_4_), channel_id=1, source_target_pairs={{0,1},{1,0},{2,3},{3,2},{4,5},{5,4},{6,7},{7,6},{8,9},{9,8},{10,11... | collective-permute-start | bytes 1327112 | tf_op jit(solution)/shard_map/ppermute | solution.py:330
  42.2 2.0 %collective-permute-start.1 = (bf16[2,576,128]{2,1,0:T(8,128)(2,1)S(1)}, bf16[2,576,128]{2,1,0:T(8,128)(2,1)}, u32[]{:S(2)}, u32[]{:S(2)}) collective-permute-start(bf16[2,576,128]{2,1,0:T(8,128)(2,1)S(1)} %pad_maximum_fusion.1.refs_0_), channel_id=1, source_target_pairs={{0,1},{1,0},{2,3},{3,2},{4,5},{5,4},{6,7},{7,6},{8,9},{9,8},{10,11... | collective-permute-start | bytes 884744 | tf_op jit(solution)/shard_map/ppermute | solution.py:330
  82.2 44.3 %all-to-all-start.2 = ((bf16[8,1408,128]{2,1,0:T(8,128)(2,1)}), bf16[8,1408,128]{2,1,0:T(8,128)(2,1)S(1)}, u32[]{:S(2)}, u32[]{:S(2)}) async-start(bf16[8,1408,128]{2,1,0:T(8,128)(2,1)} %get-tuple-element.17), calls=%async_computation.2 | async-start | bytes 5767168 | tf_op jit(solution)/shard_map/all_to_all | solution.py:353
  89.6 1.5 %collective-permute-start.8 = (bf16[576,128]{1,0:T(8,128)(2,1)S(1)}, bf16[576,128]{1,0:T(8,128)(2,1)S(1)}, u32[]{:S(2)}, u32[]{:S(2)}) collective-permute-start(bf16[576,128]{1,0:T(8,128)(2,1)S(1)} %get-tuple-element.22), channel_id=1, source_target_pairs={{0,1},{1,0},{2,3},{3,2},{4,5},{5,4},{6,7},{7,6},{8,9},{9,8},{10,11... | collective-permute-start | bytes 442376 | tf_op jit(solution)/shard_map/ppermute | solution.py:334
  91.1 7.2 %collective-permute-start.11 = (bf16[576,128]{1,0:T(8,128)(2,1)S(1)}, bf16[576,128]{1,0:T(8,128)(2,1)S(1)}, u32[]{:S(2)}, u32[]{:S(2)}) collective-permute-start(bf16[576,128]{1,0:T(8,128)(2,1)S(1)} %add_convert_fusion.2), channel_id=1, source_target_pairs={{6,0},{7,1},{0,2},{1,3},{2,4},{3,5},{4,6},{5,7},{14,8},{15,9},{8,1... | collective-permute-start | bytes 442376 | tf_op jit(solution)/shard_map/ppermute | solution.py:335
  92.7 8.1 %collective-permute-start.10 = (bf16[576,128]{1,0:T(8,128)(2,1)S(1)}, bf16[576,128]{1,0:T(8,128)(2,1)S(1)}, u32[]{:S(2)}, u32[]{:S(2)}) collective-permute-start(bf16[576,128]{1,0:T(8,128)(2,1)S(1)} %add_convert_fusion.2), channel_id=1, source_target_pairs={{2,0},{3,1},{4,2},{5,3},{6,4},{7,5},{0,6},{1,7},{10,8},{11,9},{12,... | collective-permute-start | bytes 442376 | tf_op jit(solution)/shard_map/ppermute | solution.py:335
  94.4 8.0 %collective-permute-start.9 = (bf16[576,128]{1,0:T(8,128)(2,1)S(1)}, bf16[576,128]{1,0:T(8,128)(2,1)S(1)}, u32[]{:S(2)}, u32[]{:S(2)}) collective-permute-start(bf16[576,128]{1,0:T(8,128)(2,1)S(1)} %add_convert_fusion.2), channel_id=1, source_target_pairs={{4,0},{5,1},{6,2},{7,3},{0,4},{1,5},{2,6},{3,7},{12,8},{13,9},{14,... | collective-permute-start | bytes 442376 | tf_op jit(solution)/shard_map/ppermute | solution.py:335
  102.5 20.1 %collective-permute-start.12 = (bf16[576,128]{1,0:T(8,128)(2,1)S(1)}, bf16[576,128]{1,0:T(8,128)(2,1)S(1)}, u32[]{:S(2)}, u32[]{:S(2)}) collective-permute-start(bf16[576,128]{1,0:T(8,128)(2,1)S(1)} %add_convert_fusion.1), channel_id=1, source_target_pairs={{0,8},{1,9},{2,10},{3,11},{4,12},{5,13},{6,14},{7,15},{8,0},{9,1},... | collective-permute-start | bytes 442376 | tf_op jit(solution)/shard_map/ppermute | solution.py:337
  122.6 1.5 %collective-permute-start.13 = (bf16[576,128]{1,0:T(8,128)(2,1)S(1)}, bf16[576,128]{1,0:T(8,128)(2,1)S(1)}, u32[]{:S(2)}, u32[]{:S(2)}) collective-permute-start(bf16[576,128]{1,0:T(8,128)(2,1)S(1)} %add_convert_fusion), channel_id=1, source_target_pairs={{0,1},{1,0},{2,3},{3,2},{4,5},{5,4},{6,7},{7,6},{8,9},{9,8},{10,11... | collective-permute-start | bytes 442376 | tf_op jit(solution)/shard_map/ppermute | solution.py:355

commit v4 on v3

--- a/solution.py
+++ b/solution.py
@@ -27,7 +27,7 @@
 VMEM = pl.BlockSpec(memory_space=pltpu.VMEM)
 SMEM = pl.BlockSpec(memory_space=pltpu.SMEM)
 HBM = pl.BlockSpec(memory_space=pltpu.HBM)
-BIG = pltpu.CompilerParams(vmem_limit_bytes=28 * 1024 * 1024)
+BIG = pltpu.CompilerParams(vmem_limit_bytes=34 * 1024 * 1024)
 PARAMS = pltpu.CompilerParams(vmem_limit_bytes=14 * 1024 * 1024)
 
 
@@ -78,8 +78,8 @@
 
 
 def head_kernel(order, place, recv, *refs):
-    latents, (uk_all, uv_all, keys, rest) = refs[:6], refs[6:10]
-    uk, uv, val, qf, go, kf, kt, vf, gk, gv, gq, grads_w, grads_q, sems = refs[10:]
+    latents, (uk_all, uv_all, keys, rest) = refs[:4], refs[4:8]
+    uk, uv, val, qf, go, kf, kt, vf, gk, gv, gq, ds, pb, grads_w, grads_q, sems = refs[8:]
     column = pl.ds(pl.multiple_of(place[0] * NOPE, NOPE), NOPE)
     uk_copy = pltpu.make_async_copy(uk_all.at[:, column], uk, sems.at[0])
     uv_copy = pltpu.make_async_copy(uv_all.at[:, column], uv, sems.at[1])
@@ -92,10 +92,10 @@
         return pl.ds(pl.multiple_of(order[s] * GROUP, GROUP), GROUP)
 
     for rc in range(2):
-        pair, trio, trio_z = latents[rc::2]
-        pieces = [(0, 0, pair, 0), (0, 1, pair, 1)]
-        for t, dy in enumerate((3, 1, 2)):
-            pieces += [(dy, 0, trio, t), (dy, 1, trio_z, t)]
+        quad, quad_z = latents[rc::2]
+        pieces = []
+        for t, dy in enumerate((0, 3, 1, 2)):
+            pieces += [(dy, 0, quad, t), (dy, 1, quad_z, t)]
         for dy, rz, src, t in pieces:
             c = lax.rem(y + dy, 4) * 2 + lax.rem(z + rz, 2)
             cols = at(c * 2 + lax.rem(core + rc, 2))
@@ -110,38 +110,36 @@
 
     uk_copy.wait()
     uv_copy.wait()
-    ukt = jnp.transpose(uk[...].astype(F32)).astype(BF16)
-    uvt = jnp.transpose(uv[...].astype(F32)).astype(BF16)
+    ukt = jnp.transpose(uk[...])
+    uvt = jnp.transpose(uv[...])
     for p in range(BLOCKS):
         rows = slice(p * BLOCK, (p + 1) * BLOCK)
         latent = val[:, rows]
         k_t = nn(ukt, latent)
         kt[:NOPE, rows] = k_t.astype(BF16)
-        kf[rows, :NOPE] = jnp.transpose(k_t).astype(BF16)
-        kf[rows, NOPE:] = jnp.transpose(kt[NOPE:, rows].astype(F32)).astype(BF16)
-        vf[rows, :] = jnp.transpose(nn(uvt, latent)).astype(BF16)
+        kf[rows, :] = jnp.transpose(kt[:, rows])
+        vf[rows, :] = jnp.transpose(nn(uvt, latent).astype(BF16))
 
     factor = SCALE * math.log2(math.e)
     key_at = lax.broadcasted_iota(jnp.int32, (BLOCK, BLOCK), 0)
     query_at = lax.broadcasted_iota(jnp.int32, (BLOCK, BLOCK), 1)
     seen = key_at <= query_at
     def products(i):
-        mine = slice(i * BLOCK, (i + 1) * BLOCK)
-        scores, grads = [], []
-        for j in range(i + 1):
-            rows = slice(j * BLOCK, (j + 1) * BLOCK)
-            s = nt(kf[rows, :], qf[mine, :]) * factor
-            scores.append(jnp.where(seen, s, -jnp.inf) if j == i else s)
-            grads.append(nt(vf[rows, :], go[mine, :]))
-        return scores, grads
-
+        mine, n = slice(i * BLOCK, (i + 1) * BLOCK), (i + 1) * BLOCK
+        return nt(kf[:n, :], qf[mine, :]), nt(vf[:n, :], go[mine, :])
+
+    gk[...] = jnp.zeros_like(gk)
+    gv[...] = jnp.zeros_like(gv)
     ahead = products(0)
     for i in range(BLOCKS):
-        mine = slice(i * BLOCK, (i + 1) * BLOCK)
-        q_i, g_i = qf[mine, :], go[mine, :]
-        scores, grads = ahead
+        mine, n = slice(i * BLOCK, (i + 1) * BLOCK), (i + 1) * BLOCK
+        all_scores, all_grads = ahead
         if i + 1 < BLOCKS:
             ahead = products(i + 1)
+        chunks = [slice(j * BLOCK, (j + 1) * BLOCK) for j in range(i + 1)]
+        scores = [all_scores[c] * factor for c in chunks]
+        scores[i] = jnp.where(seen, scores[i], -jnp.inf)
+        grads = [all_grads[c] for c in chunks]
         top = functools.reduce(jnp.maximum, [jnp.max(s, axis=0, keepdims=True) for s in scores])
         expo = [jnp.exp2(s - top) for s in scores]
         total = functools.reduce(jnp.add, [jnp.sum(e, axis=0, keepdims=True) for e in expo])
@@ -149,22 +147,13 @@
         delta = functools.reduce(
             jnp.add, [jnp.sum(e * d, axis=0, keepdims=True) for e, d in zip(expo, grads)]
         ) * inverse
-        acc = None
-        for j in range(i + 1):
-            rows = slice(j * BLOCK, (j + 1) * BLOCK)
-            probs = expo[j] * inverse
-            ds = (probs * (grads[j] - delta)).astype(BF16)
-            part = nn(kt[:, rows], ds)
-            acc = part if acc is None else acc + part
-            to_k = nn(ds, q_i)
-            to_v = nn(probs.astype(BF16), g_i)
-            if j == i:
-                gk[rows, :] = to_k
-                gv[rows, :] = to_v
-            else:
-                gk[rows, :] += to_k
-                gv[rows, :] += to_v
-        gq[mine, :] = jnp.transpose(acc) * SCALE
+        for c, e, d in zip(chunks, expo, grads):
+            probs = e * inverse
+            pb[i % 2, c, :] = probs.astype(BF16)
+            ds[i % 2, c, :] = (probs * (d - delta)).astype(BF16)
+        gk[:n, :] += nn(ds[i % 2, :n, :], qf[mine, :])
+        gv[:n, :] += nn(pb[i % 2, :n, :], go[mine, :])
+        gq[mine, :] = jnp.transpose(nn(kt[:, :n], ds[i % 2, :n, :])) * SCALE
 
     gkb = (gk[...] * SCALE).astype(BF16)
     gvb = gv[...].astype(BF16)
@@ -208,7 +197,7 @@
             pltpu.VMEM((CTX, 640, 128), BF16),
             pltpu.HBM((CTX, 1408, 128), BF16),
         ),
-        in_specs=[SMEM, SMEM] + [VMEM] * 7 + [HBM, HBM],
+        in_specs=[SMEM, SMEM] + [VMEM] * 5 + [HBM, HBM],
         out_specs=(VMEM, HBM),
         scratch_shapes=[
             pltpu.VMEM((LATENT, NOPE), BF16),
@@ -222,6 +211,8 @@
             pltpu.VMEM((TOKENS, NOPE + ROPE), F32),
             pltpu.VMEM((TOKENS, VHEAD), F32),
             pltpu.VMEM((TOKENS, NOPE + ROPE), F32),
+            pltpu.VMEM((2, TOKENS, BLOCK), BF16),
+            pltpu.VMEM((2, TOKENS, BLOCK), BF16),
             pltpu.VMEM((2 * LATENT, 128), BF16),
             pltpu.VMEM((CTX, 384, 128), BF16),
             pltpu.SemaphoreType.DMA((2 + 2 * CTX,)),
@@ -325,8 +316,9 @@
     return [((h & 8) + ((h // 2 + step) % 4) * 2 + h % 2, h) for h in range(HEAD)]
 
 
-def gather_latent(half, other, trio):
-    found = (jnp.stack([half, other]), trio, lax.ppermute(trio, "ctx", ZLO_SWAP))
+def gather_latent(half, along):
+    quad = jnp.stack([half, *along])
+    found = (quad, lax.ppermute(quad, "ctx", ZLO_SWAP))
     return [part for f in found for part in (f, lax.ppermute(f, "head", CORE_SWAP))]
 
 
@@ -342,10 +334,9 @@
     core = lax.axis_index("head") % 2
     place = jnp.stack([lax.axis_index("ctx"), core]).astype(jnp.int32)
     half = lax.dynamic_slice_in_dim(kv_latent.T, core * GROUP, GROUP, 1)
-    other = lax.ppermute(half, "ctx", ZLO_SWAP)
-    trio = jnp.stack([lax.ppermute(half, "ctx", from_y(d)) for d in (3, 1, 2)])
-    packed = pack(q_nope, q_rope, grad_out)
-    latents = gather_latent(half, other, trio)
+    along = [lax.ppermute(half, "ctx", from_y(d)) for d in (3, 1, 2)]
+    packed, *along = lax.optimization_barrier((pack(q_nope, q_rope, grad_out), *along))
+    latents = gather_latent(half, along)
     recv = lax.all_to_all(packed, "ctx", 0, 0, tiled=True)
     keys, rest = head_call(group_order, place, recv, latents, w_uk, w_uv)
     keys = lax.all_to_all(keys, "ctx", 0, 0, tiled=True)

time: 130 us -> 128 us (0.985)
  waiting for transfers between devices: 54.6 us -> 52.6 us
    ppermute x5 -> x4, waiting for transfers between devices: 26 us -> 23.8 us  [the longest x1 20.7 us: gather_latent(): found = (quad, lax.ppermute(quad, 'ctx', ZLO_SWAP))]
    all_to_all x1, waiting for transfers between devices: 0.01 us -> 1.67 us  [on_device(): recv = lax.all_to_all(packed, 'ctx', 0, 0, tiled=True)]
    ppermute x5 -> x4, starting transfers between devices: 7.48 us -> 7.43 us  [the longest x3 5.38 us: on_device(): along = [lax.ppermute(half, 'ctx', from_y(d)) for d in (3, 1, 2)]]
  transfers between devices with their start and end apart: 16 -> 14, of which waited for: 11 -> 13; matrix products, arithmetic and copies ran while one was open for 1% -> 1% of each run, Pallas kernels for 5% -> 5%
where the time goes in v4:
time: 128 us; the launch traced here: 127 us
  waiting for transfers between devices  52.6 us (41%)
  starting transfers between devices  24.1 us (19%)
  blocking collectives  23.9 us (19%)
  Pallas kernels  23.8 us (19%)
    all_to_all x1, blocking collectives, on_device(): keys = lax.all_to_all(keys, 'ctx', 0, 0, tiled=True)  23.9 us
    ppermute x1, waiting for transfers between devices, gather_latent(): found = (quad, lax.ppermute(quad, 'ctx', ZLO_SWAP))  20.7 us
    ppermute x1, waiting for transfers between devices, sum_heads(): far = lax.ppermute(quad, 'head', ZHI_SWAP)  16.6 us
    pallas_call x1, Pallas kernels, head_call(): pl.pallas_call(head_kernel, out_shape=(pltpu.VMEM((CTX, 640, 128), BF16),...  15 us
    ppermute x3, waiting for transfers between devices, sum_heads(): lax.ppermute(pair, 'head', from_x(d)).astype(F32)  6.21 us
    ppermute x3, starting transfers between devices, on_device(): along = [lax.ppermute(half, 'ctx', from_y(d)) for d in (3, 1, 2)]  5.38 us
    ppermute x3, starting transfers between devices, sum_heads(): lax.ppermute(pair, 'head', from_x(d)).astype(F32)  5.11 us
    all_to_all x1, starting transfers between devices, on_device(): rest = lax.all_to_all(rest, 'ctx', 0, 0, tiled=True)  3.86 us
  transfers between devices with their start and end apart: 14, of which 13 were waited for; matrix products, arithmetic and copies ran while one was open for 1% of the time, Pallas kernels for 5%

profile of v4, /device:TPU:0, one launch (start us, length us, event | category | flops | bytes accessed | tf_op | source)
XLA Modules:
  0.0 127.3 jit_solution(11039957959985187345)
XLA Ops:
  1.6 3.4 %collective-permute-start.2 = (bf16[576,128]{1,0:T(8,128)(2,1)S(1)}, bf16[576,128]{1,0:T(8,128)(2,1)S(1)}, u32[]{:S(2)}, u32[]{:S(2)}) collective-permute-start(bf16[576,128]{1,0:T(8,128)(2,1)S(1)} %get-tuple-element.36), channel_id=1, source_target_pairs={{64,0},{80,16},{96,32},{112,48},{0,64},{16,80},{32,96},{48,112},{6... | collective-permute-start | bytes 442376 | tf_op jit(solution)/shard_map/ppermute | solution.py:337
  5.0 1.1 collective-permute-start.1
  7.0 2.5 %pack.1 = bf16[8,640,128]{2,1,0:T(8,128)(2,1)} custom-call(bf16[256,1024]{1,0:T(8,128)(2,1)} %q.1, bf16[256,512]{1,0:T(8,128)(2,1)} %r.1, bf16[256,1024]{1,0:T(8,128)(2,1)} %g.1), custom_call_target="tpu_custom_call" | custom-call | tf_op jit(solution)/shard_map/pack/pallas_call | solution.py:69
  9.8 2.6 %collective-permute-done.1 = bf16[576,128]{1,0:T(8,128)(2,1)S(1)} collective-permute-done((bf16[576,128]{1,0:T(8,128)(2,1)S(1)}, bf16[576,128]{1,0:T(8,128)(2,1)S(1)}, u32[]{:S(2)}, u32[]{:S(2)}) %collective-permute-start.1) | collective-permute-done | bytes 147488 | tf_op jit(solution)/shard_map/ppermute | solution.py:337
  12.7 2.1 %collective-permute-start.4 = (bf16[4,576,128]{2,1,0:T(8,128)(2,1)S(1)}, bf16[4,576,128]{2,1,0:T(8,128)(2,1)S(1)}, u32[]{:S(2)}, u32[]{:S(2)}) collective-permute-start(bf16[4,576,128]{2,1,0:T(8,128)(2,1)S(1)} %pad_maximum_fusion.refs_0_), channel_id=1, source_target_pairs={{0,16},{16,0},{32,48},{48,32},{64,80},{80,64},{96,112},{112,96},{1... | collective-permute-start | bytes 1769480 | tf_op jit(solution)/shard_map/ppermute | solution.py:321
  14.7 3.8 %all-to-all-start = ((bf16[8,640,128]{2,1,0:T(8,128)(2,1)}), bf16[8,640,128]{2,1,0:T(8,128)(2,1)S(1)}, u32[]{:S(2)}, u32[]{:S(2)}) async-start(bf16[8,640,128]{2,1,0:T(8,128)(2,1)} %pack.1), calls=%async_computation | async-start | bytes 2621440 | tf_op jit(solution)/shard_map/all_to_all | solution.py:340
  18.6 20.7 %collective-permute-done.4.refs_2_ = bf16[4,576,128]{2,1,0:T(8,128)(2,1)S(1)} collective-permute-done((bf16[4,576,128]{2,1,0:T(8,128)(2,1)S(1)}, bf16[4,576,128]{2,1,0:T(8,128)(2,1)S(1)}, u32[]{:S(2)}, u32[]{:S(2)}) %collective-permute-start.4) | collective-permute-done | bytes 589856 | tf_op jit(solution)/shard_map/ppermute | solution.py:321
  39.3 1.7 %all-to-all-done.recv = bf16[8,640,128]{2,1,0:T(8,128)(2,1)S(1)} async-done(((bf16[8,640,128]{2,1,0:T(8,128)(2,1)}), bf16[8,640,128]{2,1,0:T(8,128)(2,1)S(1)}, u32[]{:S(2)}, u32[]{:S(2)}) %all-to-all-start) | async-done | bytes 1310752 | tf_op jit(solution)/shard_map/all_to_all | solution.py:340
  41.4 15.0 %head.1 = (bf16[8,640,128]{2,1,0:T(8,128)(2,1)S(1)}, bf16[8,1408,128]{2,1,0:T(8,128)(2,1)}) custom-call(s32[16]{0:T(128)S(1)} %copy-done, s32[2]{0:T(128)S(1)} %pad_add_fusion.place, bf16[8,640,128]{2,1,0:T(8,128)(2,1)S(1)} %all-to-all-done.recv, bf16[4,576,128]{2,1,0:T(8,128)(2,1)S(1)} %pad_maximum_fusion.refs_0_, ...), custom_call_target="tpu_custom_call" | custom-call | tf_op jit(solution)/shard_map/head/pallas_call | solution.py:194
  56.4 23.9 %all_to_all.15.back_all = bf16[8,640,128]{2,1,0:T(8,128)(2,1)} all-to-all(bf16[8,640,128]{2,1,0:T(8,128)(2,1)S(1)} %get-tuple-element.23), channel_id=1, replica_groups=mesh['ctx'=8,'head'=16] {'ctx'}, dimensions={0} | all-to-all | bytes 2621440 | tf_op jit(solution)/shard_map/all_to_all | solution.py:342
  80.3 3.9 %all-to-all-start.2 = ((bf16[8,1408,128]{2,1,0:T(8,128)(2,1)}), bf16[8,1408,128]{2,1,0:T(8,128)(2,1)S(1)}, u32[]{:S(2)}, u32[]{:S(2)}) async-start(bf16[8,1408,128]{2,1,0:T(8,128)(2,1)} %get-tuple-element.25), calls=%async_computation.2 | async-start | bytes 5767168 | tf_op jit(solution)/shard_map/all_to_all | solution.py:344
  84.1 3.7 %post.1 = (f32[576,128]{1,0:T(8,128)S(1)}, bf16[576,128]{1,0:T(8,128)(2,1)S(1)}) custom-call(s32[2]{0:T(128)S(1)} %pad_add_fusion.place, bf16[8,640,128]{2,1,0:T(8,128)(2,1)} %all_to_all.15.back_all, bf16[512,1024]{1,0:T(8,128)(2,1)} %uk_all.1, bf16[512,1024]{1,0:T(8,128)(2,1)} %uv_all.1), custom_call_target="tpu_custom_call" | custom-call | tf_op jit(solution)/shard_map/post/pallas_call | solution.py:250
  88.0 1.4 %collective-permute-done.6 = bf16[576,128]{1,0:T(8,128)(2,1)S(1)} collective-permute-done((bf16[576,128]{1,0:T(8,128)(2,1)S(1)}, bf16[576,128]{1,0:T(8,128)(2,1)S(1)}, u32[]{:S(2)}, u32[]{:S(2)}) %collective-permute-start.6) | collective-permute-done | bytes 147488 | tf_op jit(solution)/shard_map/ppermute | solution.py:326
  89.4 1.6 %collective-permute-start.9 = (bf16[576,128]{1,0:T(8,128)(2,1)S(1)}, bf16[576,128]{1,0:T(8,128)(2,1)S(1)}, u32[]{:S(2)}, u32[]{:S(2)}) collective-permute-start(bf16[576,128]{1,0:T(8,128)(2,1)S(1)} %add_convert_fusion.2), channel_id=1, source_target_pairs={{6,0},{7,1},{0,2},{1,3},{2,4},{3,5},{4,6},{5,7},{14,8},{15,9},{8,1... | collective-permute-start | bytes 442376 | tf_op jit(solution)/shard_map/ppermute | solution.py:327
  90.9 1.7 %collective-permute-start.8 = (bf16[576,128]{1,0:T(8,128)(2,1)S(1)}, bf16[576,128]{1,0:T(8,128)(2,1)S(1)}, u32[]{:S(2)}, u32[]{:S(2)}) collective-permute-start(bf16[576,128]{1,0:T(8,128)(2,1)S(1)} %add_convert_fusion.2), channel_id=1, source_target_pairs={{2,0},{3,1},{4,2},{5,3},{6,4},{7,5},{0,6},{1,7},{10,8},{11,9},{12,... | collective-permute-start | bytes 442376 | tf_op jit(solution)/shard_map/ppermute | solution.py:327
  92.7 1.8 %collective-permute-start.7 = (bf16[576,128]{1,0:T(8,128)(2,1)S(1)}, bf16[576,128]{1,0:T(8,128)(2,1)S(1)}, u32[]{:S(2)}, u32[]{:S(2)}) collective-permute-start(bf16[576,128]{1,0:T(8,128)(2,1)S(1)} %add_convert_fusion.2), channel_id=1, source_target_pairs={{4,0},{5,1},{6,2},{7,3},{0,4},{1,5},{2,6},{3,7},{12,8},{13,9},{14,... | collective-permute-start | bytes 442376 | tf_op jit(solution)/shard_map/ppermute | solution.py:327
  94.5 2.1 %collective-permute-done.9 = bf16[576,128]{1,0:T(8,128)(2,1)S(1)} collective-permute-done((bf16[576,128]{1,0:T(8,128)(2,1)S(1)}, bf16[576,128]{1,0:T(8,128)(2,1)S(1)}, u32[]{:S(2)}, u32[]{:S(2)}) %collective-permute-start.9) | collective-permute-done | bytes 147488 | tf_op jit(solution)/shard_map/ppermute | solution.py:327
  96.6 2.5 %collective-permute-done.8 = bf16[576,128]{1,0:T(8,128)(2,1)S(1)} collective-permute-done((bf16[576,128]{1,0:T(8,128)(2,1)S(1)}, bf16[576,128]{1,0:T(8,128)(2,1)S(1)}, u32[]{:S(2)}, u32[]{:S(2)}) %collective-permute-start.8) | collective-permute-done | bytes 147488 | tf_op jit(solution)/shard_map/ppermute | solution.py:327
  99.0 1.7 %collective-permute-done.7 = bf16[576,128]{1,0:T(8,128)(2,1)S(1)} collective-permute-done((bf16[576,128]{1,0:T(8,128)(2,1)S(1)}, bf16[576,128]{1,0:T(8,128)(2,1)S(1)}, u32[]{:S(2)}, u32[]{:S(2)}) %collective-permute-start.7) | collective-permute-done | bytes 147488 | tf_op jit(solution)/shard_map/ppermute | solution.py:327
  100.8 3.7 %collective-permute-start.10 = (bf16[576,128]{1,0:T(8,128)(2,1)S(1)}, bf16[576,128]{1,0:T(8,128)(2,1)S(1)}, u32[]{:S(2)}, u32[]{:S(2)}) collective-permute-start(bf16[576,128]{1,0:T(8,128)(2,1)S(1)} %add_convert_fusion.1), channel_id=1, source_target_pairs={{0,8},{1,9},{2,10},{3,11},{4,12},{5,13},{6,14},{7,15},{8,0},{9,1},... | collective-permute-start | bytes 442376 | tf_op jit(solution)/shard_map/ppermute | solution.py:329
  104.4 16.6 %collective-permute-done.10 = bf16[576,128]{1,0:T(8,128)(2,1)S(1)} collective-permute-done((bf16[576,128]{1,0:T(8,128)(2,1)S(1)}, bf16[576,128]{1,0:T(8,128)(2,1)S(1)}, u32[]{:S(2)}, u32[]{:S(2)}) %collective-permute-start.10) | collective-permute-done | bytes 147488 | tf_op jit(solution)/shard_map/ppermute | solution.py:329
  121.2 1.4 %collective-permute-done.11 = bf16[576,128]{1,0:T(8,128)(2,1)S(1)} collective-permute-done((bf16[576,128]{1,0:T(8,128)(2,1)S(1)}, bf16[576,128]{1,0:T(8,128)(2,1)S(1)}, u32[]{:S(2)}, u32[]{:S(2)}) %collective-permute-start.11) | collective-permute-done | bytes 147488 | tf_op jit(solution)/shard_map/ppermute | solution.py:346
  123.4 1.2 all-to-all-done.2.rest
  124.6 2.5 %finish.1 = (bf16[256,1024]{1,0:T(8,128)(2,1)}, bf16[256,512]{1,0:T(8,128)(2,1)}, f32[512,1024]{1,0:T(8,128)}, f32[512,1024]{1,0:T(8,128)}) custom-call(bf16[8,1408,128]{2,1,0:T(8,128)(2,1)S(1)} %all-to-all-done.2.rest), custom_call_target="tpu_custom_call" | custom-call | tf_op jit(solution)/shard_map/finish/pallas_call | solution.py:295
  (19 shorter events, 4.1 us)
Async XLA Ops:
  1.6 8.2 %collective-permute-start.2 = (bf16[576,128]{1,0:T(8,128)(2,1)S(1)}, bf16[576,128]{1,0:T(8,128)(2,1)S(1)}, u32[]{:S(2)}, u32[]{:S(2)}) collective-permute-start(bf16[576,128]{1,0:T(8,128)(2,1)S(1)} %get-tuple-element.36), channel_id=1, source_target_pairs={{64,0},{80,16},{96,32},{112,48},{0,64},{16,80},{32,96},{48,112},{6... | collective-permute-start | bytes 442376 | tf_op jit(solution)/shard_map/ppermute | solution.py:337
  5.0 7.4 %collective-permute-start.1 = (bf16[576,128]{1,0:T(8,128)(2,1)S(1)}, bf16[576,128]{1,0:T(8,128)(2,1)S(1)}, u32[]{:S(2)}, u32[]{:S(2)}) collective-permute-start(bf16[576,128]{1,0:T(8,128)(2,1)S(1)} %get-tuple-element.36), channel_id=1, source_target_pairs={{32,0},{48,16},{64,32},{80,48},{96,64},{112,80},{0,96},{16,112},{3... | collective-permute-start | bytes 442376 | tf_op jit(solution)/shard_map/ppermute | solution.py:337
  6.0 6.6 %collective-permute-start = (bf16[576,128]{1,0:T(8,128)(2,1)S(1)}, bf16[576,128]{1,0:T(8,128)(2,1)S(1)}, u32[]{:S(2)}, u32[]{:S(2)}) collective-permute-start(bf16[576,128]{1,0:T(8,128)(2,1)S(1)} %get-tuple-element.36), channel_id=1, source_target_pairs={{96,0},{112,16},{0,32},{16,48},{32,64},{48,80},{64,96},{80,112},{9... | collective-permute-start | bytes 442376 | tf_op jit(solution)/shard_map/ppermute | solution.py:337
  9.5 31.9 %copy-start = (s32[16]{0:T(128)S(1)}, s32[16]{0:T(128)}, u32[]{:S(2)}) copy-start(s32[16]{0:T(128)} %order.1) | copy-start | bytes 196
  12.7 26.6 %collective-permute-start.4 = (bf16[4,576,128]{2,1,0:T(8,128)(2,1)S(1)}, bf16[4,576,128]{2,1,0:T(8,128)(2,1)S(1)}, u32[]{:S(2)}, u32[]{:S(2)}) collective-permute-start(bf16[4,576,128]{2,1,0:T(8,128)(2,1)S(1)} %pad_maximum_fusion.refs_0_), channel_id=1, source_target_pairs={{0,16},{16,0},{32,48},{48,32},{64,80},{80,64},{96,112},{112,96},{1... | collective-permute-start | bytes 1769480 | tf_op jit(solution)/shard_map/ppermute | solution.py:321
  14.7 26.3 %all-to-all-start = ((bf16[8,640,128]{2,1,0:T(8,128)(2,1)}), bf16[8,640,128]{2,1,0:T(8,128)(2,1)S(1)}, u32[]{:S(2)}, u32[]{:S(2)}) async-start(bf16[8,640,128]{2,1,0:T(8,128)(2,1)} %pack.1), calls=%async_computation | async-start | bytes 2621440 | tf_op jit(solution)/shard_map/all_to_all | solution.py:340
  18.6 20.8 %collective-permute-start.3 = (bf16[4,576,128]{2,1,0:T(8,128)(2,1)S(1)}, bf16[4,576,128]{2,1,0:T(8,128)(2,1)S(1)}, u32[]{:S(2)}, u32[]{:S(2)}) collective-permute-start(bf16[4,576,128]{2,1,0:T(8,128)(2,1)S(1)} %pad_maximum_fusion.refs_0_), channel_id=1, source_target_pairs={{0,1},{1,0},{2,3},{3,2},{4,5},{5,4},{6,7},{7,6},{8,9},{9,8},{10,11... | collective-permute-start | bytes 1769480 | tf_op jit(solution)/shard_map/ppermute | solution.py:322
  39.3 2.1 %collective-permute-start.5 = (bf16[4,576,128]{2,1,0:T(8,128)(2,1)S(1)}, bf16[4,576,128]{2,1,0:T(8,128)(2,1)}, u32[]{:S(2)}, u32[]{:S(2)}) collective-permute-start(bf16[4,576,128]{2,1,0:T(8,128)(2,1)S(1)} %collective-permute-done.4.refs_2_), channel_id=1, source_target_pairs={{0,1},{1,0},{2,3},{3,2},{4,5},{5,4},{6,7},{7,6},{8,9},{9,8},{10,11... | collective-permute-start | bytes 1769480 | tf_op jit(solution)/shard_map/ppermute | solution.py:322
  80.3 44.3 %all-to-all-start.2 = ((bf16[8,1408,128]{2,1,0:T(8,128)(2,1)}), bf16[8,1408,128]{2,1,0:T(8,128)(2,1)S(1)}, u32[]{:S(2)}, u32[]{:S(2)}) async-start(bf16[8,1408,128]{2,1,0:T(8,128)(2,1)} %get-tuple-element.25), calls=%async_computation.2 | async-start | bytes 5767168 | tf_op jit(solution)/shard_map/all_to_all | solution.py:344
  87.9 1.5 %collective-permute-start.6 = (bf16[576,128]{1,0:T(8,128)(2,1)S(1)}, bf16[576,128]{1,0:T(8,128)(2,1)S(1)}, u32[]{:S(2)}, u32[]{:S(2)}) collective-permute-start(bf16[576,128]{1,0:T(8,128)(2,1)S(1)} %get-tuple-element.30), channel_id=1, source_target_pairs={{0,1},{1,0},{2,3},{3,2},{4,5},{5,4},{6,7},{7,6},{8,9},{9,8},{10,11... | collective-permute-start | bytes 442376 | tf_op jit(solution)/shard_map/ppermute | solution.py:326
  89.4 7.2 %collective-permute-start.9 = (bf16[576,128]{1,0:T(8,128)(2,1)S(1)}, bf16[576,128]{1,0:T(8,128)(2,1)S(1)}, u32[]{:S(2)}, u32[]{:S(2)}) collective-permute-start(bf16[576,128]{1,0:T(8,128)(2,1)S(1)} %add_convert_fusion.2), channel_id=1, source_target_pairs={{6,0},{7,1},{0,2},{1,3},{2,4},{3,5},{4,6},{5,7},{14,8},{15,9},{8,1... | collective-permute-start | bytes 442376 | tf_op jit(solution)/shard_map/ppermute | solution.py:327
  90.9 8.1 %collective-permute-start.8 = (bf16[576,128]{1,0:T(8,128)(2,1)S(1)}, bf16[576,128]{1,0:T(8,128)(2,1)S(1)}, u32[]{:S(2)}, u32[]{:S(2)}) collective-permute-start(bf16[576,128]{1,0:T(8,128)(2,1)S(1)} %add_convert_fusion.2), channel_id=1, source_target_pairs={{2,0},{3,1},{4,2},{5,3},{6,4},{7,5},{0,6},{1,7},{10,8},{11,9},{12,... | collective-permute-start | bytes 442376 | tf_op jit(solution)/shard_map/ppermute | solution.py:327
  92.7 8.0 %collective-permute-start.7 = (bf16[576,128]{1,0:T(8,128)(2,1)S(1)}, bf16[576,128]{1,0:T(8,128)(2,1)S(1)}, u32[]{:S(2)}, u32[]{:S(2)}) collective-permute-start(bf16[576,128]{1,0:T(8,128)(2,1)S(1)} %add_convert_fusion.2), channel_id=1, source_target_pairs={{4,0},{5,1},{6,2},{7,3},{0,4},{1,5},{2,6},{3,7},{12,8},{13,9},{14,... | collective-permute-start | bytes 442376 | tf_op jit(solution)/shard_map/ppermute | solution.py:327
  100.8 20.3 %collective-permute-start.10 = (bf16[576,128]{1,0:T(8,128)(2,1)S(1)}, bf16[576,128]{1,0:T(8,128)(2,1)S(1)}, u32[]{:S(2)}, u32[]{:S(2)}) collective-permute-start(bf16[576,128]{1,0:T(8,128)(2,1)S(1)} %add_convert_fusion.1), channel_id=1, source_target_pairs={{0,8},{1,9},{2,10},{3,11},{4,12},{5,13},{6,14},{7,15},{8,0},{9,1},... | collective-permute-start | bytes 442376 | tf_op jit(solution)/shard_map/ppermute | solution.py:329
  121.1 1.5 %collective-permute-start.11 = (bf16[576,128]{1,0:T(8,128)(2,1)S(1)}, bf16[576,128]{1,0:T(8,128)(2,1)S(1)}, u32[]{:S(2)}, u32[]{:S(2)}) collective-permute-start(bf16[576,128]{1,0:T(8,128)(2,1)S(1)} %add_convert_fusion), channel_id=1, source_target_pairs={{0,1},{1,0},{2,3},{3,2},{4,5},{5,4},{6,7},{7,6},{8,9},{9,8},{10,11... | collective-permute-start | bytes 442376 | tf_op jit(solution)/shard_map/ppermute | solution.py:346

commit v5 on v4

--- a/solution.py
+++ b/solution.py
@@ -78,8 +78,8 @@
 
 
 def head_kernel(order, place, recv, *refs):
-    latents, (uk_all, uv_all, keys, rest) = refs[:4], refs[4:8]
-    uk, uv, val, qf, go, kf, kt, vf, gk, gv, gq, ds, pb, grads_w, grads_q, sems = refs[8:]
+    latents, (uk_all, uv_all, keys, rest) = refs[:8], refs[8:12]
+    uk, uv, val, qf, go, kf, kt, vf, gk, gv, gq, ds, pb, grads_w, grads_q, sems = refs[12:]
     column = pl.ds(pl.multiple_of(place[0] * NOPE, NOPE), NOPE)
     uk_copy = pltpu.make_async_copy(uk_all.at[:, column], uk, sems.at[0])
     uv_copy = pltpu.make_async_copy(uv_all.at[:, column], uv, sems.at[1])
@@ -92,15 +92,14 @@
         return pl.ds(pl.multiple_of(order[s] * GROUP, GROUP), GROUP)
 
     for rc in range(2):
-        quad, quad_z = latents[rc::2]
-        pieces = []
-        for t, dy in enumerate((0, 3, 1, 2)):
-            pieces += [(dy, 0, quad, t), (dy, 1, quad_z, t)]
-        for dy, rz, src, t in pieces:
+        early, below, above, opposite = latents[rc::2]
+        pieces = [(dy, rz, early.at[t]) for t, (dy, rz) in enumerate(((0, 0), (3, 0), (1, 0), (2, 0), (0, 1)))]
+        pieces += [(3, 1, below), (1, 1, above), (2, 1, opposite)]
+        for dy, rz, src in pieces:
             c = lax.rem(y + dy, 4) * 2 + lax.rem(z + rz, 2)
             cols = at(c * 2 + lax.rem(core + rc, 2))
-            val[:, cols] = src[t, :LATENT, :]
-            kt[NOPE:, cols] = src[t, LATENT:, :]
+            val[:, cols] = src[:LATENT, :]
+            kt[NOPE:, cols] = src[LATENT:, :]
     for s in range(GROUPS):
         c, b = s // 2, s % 2
         rows = at(s)
@@ -197,7 +196,7 @@
             pltpu.VMEM((CTX, 640, 128), BF16),
             pltpu.HBM((CTX, 1408, 128), BF16),
         ),
-        in_specs=[SMEM, SMEM] + [VMEM] * 5 + [HBM, HBM],
+        in_specs=[SMEM, SMEM] + [VMEM] * 9 + [HBM, HBM],
         out_specs=(VMEM, HBM),
         scratch_shapes=[
             pltpu.VMEM((LATENT, NOPE), BF16),
@@ -316,9 +315,10 @@
     return [((h & 8) + ((h // 2 + step) % 4) * 2 + h % 2, h) for h in range(HEAD)]
 
 
-def gather_latent(half, along):
-    quad = jnp.stack([half, *along])
-    found = (quad, lax.ppermute(quad, "ctx", ZLO_SWAP))
+def gather_latent(half, below, above, far_off, other):
+    found = [jnp.stack([half, below, above, far_off, other])]
+    found += [lax.ppermute(other, "ctx", from_y(d)) for d in (3, 1)]
+    found.append(lax.ppermute(far_off, "ctx", ZLO_SWAP))
     return [part for f in found for part in (f, lax.ppermute(f, "head", CORE_SWAP))]
 
 
@@ -334,9 +334,10 @@
     core = lax.axis_index("head") % 2
     place = jnp.stack([lax.axis_index("ctx"), core]).astype(jnp.int32)
     half = lax.dynamic_slice_in_dim(kv_latent.T, core * GROUP, GROUP, 1)
-    along = [lax.ppermute(half, "ctx", from_y(d)) for d in (3, 1, 2)]
-    packed, *along = lax.optimization_barrier((pack(q_nope, q_rope, grad_out), *along))
-    latents = gather_latent(half, along)
+    blocks = [half] + [lax.ppermute(half, "ctx", from_y(d)) for d in (3, 1, 2)]
+    blocks.append(lax.ppermute(half, "ctx", ZLO_SWAP))
+    packed, *blocks = lax.optimization_barrier((pack(q_nope, q_rope, grad_out), *blocks))
+    latents = gather_latent(*blocks)
     recv = lax.all_to_all(packed, "ctx", 0, 0, tiled=True)
     keys, rest = head_call(group_order, place, recv, latents, w_uk, w_uv)
     keys = lax.all_to_all(keys, "ctx", 0, 0, tiled=True)

time: 128 us -> 126 us (0.984)
  waiting for transfers between devices: 52.6 us -> 45.9 us
  starting transfers between devices: 24.1 us -> 28.6 us
  local copies, waits for them, and re-layouts: 0.96 us -> 2.88 us
    ppermute x4 -> x7, waiting for transfers between devices: 23.8 us -> 16.8 us  [the longest x1 12.6 us: gather_latent(): found.append(lax.ppermute(far_off, 'ctx', ZLO_SWAP))]
    ppermute x4 -> x7, starting transfers between devices: 7.43 us -> 12.1 us  [the longest x3 5.22 us: on_device(): blocks = [half] + [lax.ppermute(half, 'ctx', from_y(d)) for d in (3, 1, 2)]]
    unnamed x2 -> x8, local copies, waits for them, and re-layouts: 0.01 us -> 1.94 us
    all_to_all x1, waiting for transfers between devices: 1.67 us -> 0.01 us  [on_device(): recv = lax.all_to_all(packed, 'ctx', 0, 0, tiled=True)]
  transfers between devices with their start and end apart: 14 -> 19, of which waited for: 13 -> 16; matrix products, arithmetic and copies ran while one was open for 1% -> 2% of each run, Pallas kernels for 5% -> 5%
where the time goes in v5:
time: 126 us
  waiting for transfers between devices  45.9 us (36%)
  starting transfers between devices  28.6 us (23%)
  Pallas kernels  23.8 us (19%)
  blocking collectives  22.7 us (18%)
  local copies, waits for them, and re-layouts  2.88 us (2%)
    all_to_all x1, blocking collectives, on_device(): keys = lax.all_to_all(keys, 'ctx', 0, 0, tiled=True)  22.7 us
    ppermute x1, waiting for transfers between devices, sum_heads(): far = lax.ppermute(quad, 'head', ZHI_SWAP)  16.9 us
    pallas_call x1, Pallas kernels, head_call(): pl.pallas_call(head_kernel, out_shape=(pltpu.VMEM((CTX, 640, 128), BF16),...  15 us
    ppermute x1, waiting for transfers between devices, gather_latent(): found.append(lax.ppermute(far_off, 'ctx', ZLO_SWAP))  12.6 us
    ppermute x3, waiting for transfers between devices, sum_heads(): lax.ppermute(pair, 'head', from_x(d)).astype(F32)  6.2 us
    ppermute x3, starting transfers between devices, on_device(): blocks = [half] + [lax.ppermute(half, 'ctx', from_y(d)) for d in (3, 1, 2)]  5.22 us
    ppermute x3, starting transfers between devices, sum_heads(): lax.ppermute(pair, 'head', from_x(d)).astype(F32)  5.11 us
    all_to_all x1, starting transfers between devices, on_device(): rest = lax.all_to_all(rest, 'ctx', 0, 0, tiled=True)  3.86 us
  transfers between devices with their start and end apart: 19, of which 16 were waited for; matrix products, arithmetic and copies ran while one was open for 2% of the time, Pallas kernels for 5%

profile of v5, /device:TPU:0, one launch (start us, length us, event | category | flops | bytes accessed | tf_op | source)
XLA Modules:
  0.0 125.9 jit_solution(14551490340445385410)
XLA Ops:
  1.6 2.1 %collective-permute-start.3 = (bf16[576,128]{1,0:T(8,128)(2,1)S(1)}, bf16[576,128]{1,0:T(8,128)(2,1)}, u32[]{:S(2)}, u32[]{:S(2)}) collective-permute-start(bf16[576,128]{1,0:T(8,128)(2,1)S(1)} %dynamic-slice_bitcast_fusion), channel_id=1, source_target_pairs={{0,16},{16,0},{32,48},{48,32},{64,80},{80,64},{96,112},{112,96},{1... | collective-permute-start | bytes 442376 | tf_op jit(solution)/shard_map/ppermute | solution.py:338
  3.7 3.2 %collective-permute-start.2 = (bf16[576,128]{1,0:T(8,128)(2,1)S(1)}, bf16[576,128]{1,0:T(8,128)(2,1)}, u32[]{:S(2)}, u32[]{:S(2)}) collective-permute-start(bf16[576,128]{1,0:T(8,128)(2,1)S(1)} %dynamic-slice_bitcast_fusion), channel_id=1, source_target_pairs={{64,0},{80,16},{96,32},{112,48},{0,64},{16,80},{32,96},{48,112},{6... | collective-permute-start | bytes 442376 | tf_op jit(solution)/shard_map/ppermute | solution.py:337
  8.9 2.5 %pack.1 = bf16[8,640,128]{2,1,0:T(8,128)(2,1)} custom-call(bf16[256,1024]{1,0:T(8,128)(2,1)} %q.1, bf16[256,512]{1,0:T(8,128)(2,1)} %r.1, bf16[256,1024]{1,0:T(8,128)(2,1)} %g.1), custom_call_target="tpu_custom_call" | custom-call | tf_op jit(solution)/shard_map/pack/pallas_call | solution.py:69
  11.7 2.3 %collective-permute-done.1 = bf16[576,128]{1,0:T(8,128)(2,1)S(1)} collective-permute-done((bf16[576,128]{1,0:T(8,128)(2,1)S(1)}, bf16[576,128]{1,0:T(8,128)(2,1)S(1)}, u32[]{:S(2)}, u32[]{:S(2)}) %collective-permute-start.1) | collective-permute-done | bytes 147488 | tf_op jit(solution)/shard_map/ppermute | solution.py:337
  14.3 3.8 %all-to-all-start = ((bf16[8,640,128]{2,1,0:T(8,128)(2,1)}), bf16[8,640,128]{2,1,0:T(8,128)(2,1)S(1)}, u32[]{:S(2)}, u32[]{:S(2)}) async-start(bf16[8,640,128]{2,1,0:T(8,128)(2,1)} %pack.1), calls=%async_computation | async-start | bytes 2621440 | tf_op jit(solution)/shard_map/all_to_all | solution.py:341
  20.2 2.1 %collective-permute-start.9 = (bf16[576,128]{1,0:T(8,128)(2,1)}, bf16[576,128]{1,0:T(8,128)(2,1)S(1)}, u32[]{:S(2)}, u32[]{:S(2)}) collective-permute-start(bf16[576,128]{1,0:T(8,128)(2,1)} %collective-permute-done.2), channel_id=1, source_target_pairs={{0,16},{16,0},{32,48},{48,32},{64,80},{80,64},{96,112},{112,96},{1... | collective-permute-start | bytes 442376 | tf_op jit(solution)/shard_map/ppermute | solution.py:321
  22.3 2.7 %collective-permute-start.7 = (bf16[576,128]{1,0:T(8,128)(2,1)}, bf16[576,128]{1,0:T(8,128)(2,1)S(1)}, u32[]{:S(2)}, u32[]{:S(2)}) collective-permute-start(bf16[576,128]{1,0:T(8,128)(2,1)} %collective-permute-done.3), channel_id=1, source_target_pairs={{32,0},{48,16},{64,32},{80,48},{96,64},{112,80},{0,96},{16,112},{3... | collective-permute-start | bytes 442376 | tf_op jit(solution)/shard_map/ppermute | solution.py:320
  25.0 12.6 %collective-permute-done.9.refs_6_ = bf16[576,128]{1,0:T(8,128)(2,1)S(1)} collective-permute-done((bf16[576,128]{1,0:T(8,128)(2,1)}, bf16[576,128]{1,0:T(8,128)(2,1)S(1)}, u32[]{:S(2)}, u32[]{:S(2)}) %collective-permute-start.9) | collective-permute-done | bytes 147488 | tf_op jit(solution)/shard_map/ppermute | solution.py:321
  40.4 15.0 %head.1 = (bf16[8,640,128]{2,1,0:T(8,128)(2,1)S(1)}, bf16[8,1408,128]{2,1,0:T(8,128)(2,1)}) custom-call(s32[16]{0:T(128)S(1)} %copy-done.1, s32[2]{0:T(128)S(1)} %pad_add_fusion.place, bf16[8,640,128]{2,1,0:T(8,128)(2,1)S(1)} %all-to-all-done.recv, bf16[5,576,128]{2,1,0:T(8,128)(2,1)S(1)} %bitcast_dynamic-update-slice_fusion.refs_0_, ...), custom_call_target="tpu_custom_call" | custom-call | tf_op jit(solution)/shard_map/head/pallas_call | solution.py:193
  55.4 22.7 %all_to_all.15.back_all = bf16[8,640,128]{2,1,0:T(8,128)(2,1)} all-to-all(bf16[8,640,128]{2,1,0:T(8,128)(2,1)S(1)} %get-tuple-element.27), channel_id=1, replica_groups=mesh['ctx'=8,'head'=16] {'ctx'}, dimensions={0} | all-to-all | bytes 2621440 | tf_op jit(solution)/shard_map/all_to_all | solution.py:343
  78.2 3.9 %all-to-all-start.2 = ((bf16[8,1408,128]{2,1,0:T(8,128)(2,1)}), bf16[8,1408,128]{2,1,0:T(8,128)(2,1)S(1)}, u32[]{:S(2)}, u32[]{:S(2)}) async-start(bf16[8,1408,128]{2,1,0:T(8,128)(2,1)} %get-tuple-element.29), calls=%async_computation.2 | async-start | bytes 5767168 | tf_op jit(solution)/shard_map/all_to_all | solution.py:345
  82.0 3.7 %post.1 = (f32[576,128]{1,0:T(8,128)S(1)}, bf16[576,128]{1,0:T(8,128)(2,1)S(1)}) custom-call(s32[2]{0:T(128)S(1)} %pad_add_fusion.place, bf16[8,640,128]{2,1,0:T(8,128)(2,1)} %all_to_all.15.back_all, bf16[512,1024]{1,0:T(8,128)(2,1)} %uk_all.1, bf16[512,1024]{1,0:T(8,128)(2,1)} %uv_all.1), custom_call_target="tpu_custom_call" | custom-call | tf_op jit(solution)/shard_map/post/pallas_call | solution.py:249
  85.9 1.4 %collective-permute-done.11 = bf16[576,128]{1,0:T(8,128)(2,1)S(1)} collective-permute-done((bf16[576,128]{1,0:T(8,128)(2,1)S(1)}, bf16[576,128]{1,0:T(8,128)(2,1)S(1)}, u32[]{:S(2)}, u32[]{:S(2)}) %collective-permute-start.11) | collective-permute-done | bytes 147488 | tf_op jit(solution)/shard_map/ppermute | solution.py:326
  87.3 1.6 %collective-permute-start.14 = (bf16[576,128]{1,0:T(8,128)(2,1)S(1)}, bf16[576,128]{1,0:T(8,128)(2,1)S(1)}, u32[]{:S(2)}, u32[]{:S(2)}) collective-permute-start(bf16[576,128]{1,0:T(8,128)(2,1)S(1)} %add_convert_fusion.2), channel_id=1, source_target_pairs={{6,0},{7,1},{0,2},{1,3},{2,4},{3,5},{4,6},{5,7},{14,8},{15,9},{8,1... | collective-permute-start | bytes 442376 | tf_op jit(solution)/shard_map/ppermute | solution.py:327
  88.8 1.7 %collective-permute-start.13 = (bf16[576,128]{1,0:T(8,128)(2,1)S(1)}, bf16[576,128]{1,0:T(8,128)(2,1)S(1)}, u32[]{:S(2)}, u32[]{:S(2)}) collective-permute-start(bf16[576,128]{1,0:T(8,128)(2,1)S(1)} %add_convert_fusion.2), channel_id=1, source_target_pairs={{2,0},{3,1},{4,2},{5,3},{6,4},{7,5},{0,6},{1,7},{10,8},{11,9},{12,... | collective-permute-start | bytes 442376 | tf_op jit(solution)/shard_map/ppermute | solution.py:327
  90.6 1.8 %collective-permute-start.12 = (bf16[576,128]{1,0:T(8,128)(2,1)S(1)}, bf16[576,128]{1,0:T(8,128)(2,1)S(1)}, u32[]{:S(2)}, u32[]{:S(2)}) collective-permute-start(bf16[576,128]{1,0:T(8,128)(2,1)S(1)} %add_convert_fusion.2), channel_id=1, source_target_pairs={{4,0},{5,1},{6,2},{7,3},{0,4},{1,5},{2,6},{3,7},{12,8},{13,9},{14,... | collective-permute-start | bytes 442376 | tf_op jit(solution)/shard_map/ppermute | solution.py:327
  92.4 2.1 %collective-permute-done.14 = bf16[576,128]{1,0:T(8,128)(2,1)S(1)} collective-permute-done((bf16[576,128]{1,0:T(8,128)(2,1)S(1)}, bf16[576,128]{1,0:T(8,128)(2,1)S(1)}, u32[]{:S(2)}, u32[]{:S(2)}) %collective-permute-start.14) | collective-permute-done | bytes 147488 | tf_op jit(solution)/shard_map/ppermute | solution.py:327
  94.5 2.5 %collective-permute-done.13 = bf16[576,128]{1,0:T(8,128)(2,1)S(1)} collective-permute-done((bf16[576,128]{1,0:T(8,128)(2,1)S(1)}, bf16[576,128]{1,0:T(8,128)(2,1)S(1)}, u32[]{:S(2)}, u32[]{:S(2)}) %collective-permute-start.13) | collective-permute-done | bytes 147488 | tf_op jit(solution)/shard_map/ppermute | solution.py:327
  96.9 1.7 %collective-permute-done.12 = bf16[576,128]{1,0:T(8,128)(2,1)S(1)} collective-permute-done((bf16[576,128]{1,0:T(8,128)(2,1)S(1)}, bf16[576,128]{1,0:T(8,128)(2,1)S(1)}, u32[]{:S(2)}, u32[]{:S(2)}) %collective-permute-start.12) | collective-permute-done | bytes 147488 | tf_op jit(solution)/shard_map/ppermute | solution.py:327
  98.7 3.5 %collective-permute-start.15 = (bf16[576,128]{1,0:T(8,128)(2,1)S(1)}, bf16[576,128]{1,0:T(8,128)(2,1)S(1)}, u32[]{:S(2)}, u32[]{:S(2)}) collective-permute-start(bf16[576,128]{1,0:T(8,128)(2,1)S(1)} %add_convert_fusion.1), channel_id=1, source_target_pairs={{0,8},{1,9},{2,10},{3,11},{4,12},{5,13},{6,14},{7,15},{8,0},{9,1},... | collective-permute-start | bytes 442376 | tf_op jit(solution)/shard_map/ppermute | solution.py:329
  102.2 16.9 %collective-permute-done.15 = bf16[576,128]{1,0:T(8,128)(2,1)S(1)} collective-permute-done((bf16[576,128]{1,0:T(8,128)(2,1)S(1)}, bf16[576,128]{1,0:T(8,128)(2,1)S(1)}, u32[]{:S(2)}, u32[]{:S(2)}) %collective-permute-start.15) | collective-permute-done | bytes 147488 | tf_op jit(solution)/shard_map/ppermute | solution.py:329
  119.2 1.4 %collective-permute-done.16 = bf16[576,128]{1,0:T(8,128)(2,1)S(1)} collective-permute-done((bf16[576,128]{1,0:T(8,128)(2,1)S(1)}, bf16[576,128]{1,0:T(8,128)(2,1)S(1)}, u32[]{:S(2)}, u32[]{:S(2)}) %collective-permute-start.16) | collective-permute-done | bytes 147488 | tf_op jit(solution)/shard_map/ppermute | solution.py:347
  121.3 1.8 %all-to-all-done.2.rest = bf16[8,1408,128]{2,1,0:T(8,128)(2,1)S(1)} async-done(((bf16[8,1408,128]{2,1,0:T(8,128)(2,1)}), bf16[8,1408,128]{2,1,0:T(8,128)(2,1)S(1)}, u32[]{:S(2)}, u32[]{:S(2)}) %all-to-all-start.2) | async-done | bytes 2883616 | tf_op jit(solution)/shard_map/all_to_all | solution.py:345
  123.2 2.5 %finish.1 = (bf16[256,1024]{1,0:T(8,128)(2,1)}, bf16[256,512]{1,0:T(8,128)(2,1)}, f32[512,1024]{1,0:T(8,128)}, f32[512,1024]{1,0:T(8,128)}) custom-call(bf16[8,1408,128]{2,1,0:T(8,128)(2,1)S(1)} %all-to-all-done.2.rest), custom_call_target="tpu_custom_call" | custom-call | tf_op jit(solution)/shard_map/finish/pallas_call | solution.py:294
  (35 shorter events, 9.5 us)
Async XLA Ops:
  0.6 1.0 copy-start
  1.6 9.8 %collective-permute-start.3 = (bf16[576,128]{1,0:T(8,128)(2,1)S(1)}, bf16[576,128]{1,0:T(8,128)(2,1)}, u32[]{:S(2)}, u32[]{:S(2)}) collective-permute-start(bf16[576,128]{1,0:T(8,128)(2,1)S(1)} %dynamic-slice_bitcast_fusion), channel_id=1, source_target_pairs={{0,16},{16,0},{32,48},{48,32},{64,80},{80,64},{96,112},{112,96},{1... | collective-permute-start | bytes 442376 | tf_op jit(solution)/shard_map/ppermute | solution.py:338
  3.7 8.0 %collective-permute-start.2 = (bf16[576,128]{1,0:T(8,128)(2,1)S(1)}, bf16[576,128]{1,0:T(8,128)(2,1)}, u32[]{:S(2)}, u32[]{:S(2)}) collective-permute-start(bf16[576,128]{1,0:T(8,128)(2,1)S(1)} %dynamic-slice_bitcast_fusion), channel_id=1, source_target_pairs={{64,0},{80,16},{96,32},{112,48},{0,64},{16,80},{32,96},{48,112},{6... | collective-permute-start | bytes 442376 | tf_op jit(solution)/shard_map/ppermute | solution.py:337
  6.9 7.1 %collective-permute-start.1 = (bf16[576,128]{1,0:T(8,128)(2,1)S(1)}, bf16[576,128]{1,0:T(8,128)(2,1)S(1)}, u32[]{:S(2)}, u32[]{:S(2)}) collective-permute-start(bf16[576,128]{1,0:T(8,128)(2,1)S(1)} %dynamic-slice_bitcast_fusion), channel_id=1, source_target_pairs={{32,0},{48,16},{64,32},{80,48},{96,64},{112,80},{0,96},{16,112},{3... | collective-permute-start | bytes 442376 | tf_op jit(solution)/shard_map/ppermute | solution.py:337
  7.9 6.4 %collective-permute-start = (bf16[576,128]{1,0:T(8,128)(2,1)S(1)}, bf16[576,128]{1,0:T(8,128)(2,1)S(1)}, u32[]{:S(2)}, u32[]{:S(2)}) collective-permute-start(bf16[576,128]{1,0:T(8,128)(2,1)S(1)} %dynamic-slice_bitcast_fusion), channel_id=1, source_target_pairs={{96,0},{112,16},{0,32},{16,48},{32,64},{48,80},{64,96},{80,112},{9... | collective-permute-start | bytes 442376 | tf_op jit(solution)/shard_map/ppermute | solution.py:337
  11.4 29.0 %copy-start.1 = (s32[16]{0:T(128)S(1)}, s32[16]{0:T(128)}, u32[]{:S(2)}) copy-start(s32[16]{0:T(128)} %order.1) | copy-start | bytes 196
  14.3 26.1 %all-to-all-start = ((bf16[8,640,128]{2,1,0:T(8,128)(2,1)}), bf16[8,640,128]{2,1,0:T(8,128)(2,1)S(1)}, u32[]{:S(2)}, u32[]{:S(2)}) async-start(bf16[8,640,128]{2,1,0:T(8,128)(2,1)} %pack.1), calls=%async_computation | async-start | bytes 2621440 | tf_op jit(solution)/shard_map/all_to_all | solution.py:341
  20.1 20.3 %collective-permute-start.4 = (bf16[5,576,128]{2,1,0:T(8,128)(2,1)S(1)}, bf16[5,576,128]{2,1,0:T(8,128)(2,1)S(1)}, u32[]{:S(2)}, u32[]{:S(2)}) collective-permute-start(bf16[5,576,128]{2,1,0:T(8,128)(2,1)S(1)} %bitcast_dynamic-update-slice_fusion.refs_0_), channel_id=1, source_target_pairs={{0,1},{1,0},{2,3},{3,2},{4,5},{5,4},{6,7},{7,6},{8,9},{9,8},{10,11... | collective-permute-start | bytes 2211848 | tf_op jit(solution)/shard_map/ppermute | solution.py:322
  20.2 17.4 %collective-permute-start.9 = (bf16[576,128]{1,0:T(8,128)(2,1)}, bf16[576,128]{1,0:T(8,128)(2,1)S(1)}, u32[]{:S(2)}, u32[]{:S(2)}) collective-permute-start(bf16[576,128]{1,0:T(8,128)(2,1)} %collective-permute-done.2), channel_id=1, source_target_pairs={{0,16},{16,0},{32,48},{48,32},{64,80},{80,64},{96,112},{112,96},{1... | collective-permute-start | bytes 442376 | tf_op jit(solution)/shard_map/ppermute | solution.py:321
  22.3 15.8 %collective-permute-start.7 = (bf16[576,128]{1,0:T(8,128)(2,1)}, bf16[576,128]{1,0:T(8,128)(2,1)S(1)}, u32[]{:S(2)}, u32[]{:S(2)}) collective-permute-start(bf16[576,128]{1,0:T(8,128)(2,1)} %collective-permute-done.3), channel_id=1, source_target_pairs={{32,0},{48,16},{64,32},{80,48},{96,64},{112,80},{0,96},{16,112},{3... | collective-permute-start | bytes 442376 | tf_op jit(solution)/shard_map/ppermute | solution.py:320
  24.9 14.0 %collective-permute-start.5 = (bf16[576,128]{1,0:T(8,128)(2,1)}, bf16[576,128]{1,0:T(8,128)(2,1)S(1)}, u32[]{:S(2)}, u32[]{:S(2)}) collective-permute-start(bf16[576,128]{1,0:T(8,128)(2,1)} %collective-permute-done.3), channel_id=1, source_target_pairs={{96,0},{112,16},{0,32},{16,48},{32,64},{48,80},{64,96},{80,112},{9... | collective-permute-start | bytes 442376 | tf_op jit(solution)/shard_map/ppermute | solution.py:320
  37.6 1.5 %collective-permute-start.10 = (bf16[576,128]{1,0:T(8,128)(2,1)S(1)}, bf16[576,128]{1,0:T(8,128)(2,1)}, u32[]{:S(2)}, u32[]{:S(2)}) collective-permute-start(bf16[576,128]{1,0:T(8,128)(2,1)S(1)} %collective-permute-done.9.refs_6_), channel_id=1, source_target_pairs={{0,1},{1,0},{2,3},{3,2},{4,5},{5,4},{6,7},{7,6},{8,9},{9,8},{10,11... | collective-permute-start | bytes 442376 | tf_op jit(solution)/shard_map/ppermute | solution.py:322
  38.1 1.5 %collective-permute-start.8 = (bf16[576,128]{1,0:T(8,128)(2,1)S(1)}, bf16[576,128]{1,0:T(8,128)(2,1)}, u32[]{:S(2)}, u32[]{:S(2)}) collective-permute-start(bf16[576,128]{1,0:T(8,128)(2,1)S(1)} %collective-permute-done.7.refs_4_), channel_id=1, source_target_pairs={{0,1},{1,0},{2,3},{3,2},{4,5},{5,4},{6,7},{7,6},{8,9},{9,8},{10,11... | collective-permute-start | bytes 442376 | tf_op jit(solution)/shard_map/ppermute | solution.py:322
  38.9 1.5 %collective-permute-start.6 = (bf16[576,128]{1,0:T(8,128)(2,1)S(1)}, bf16[576,128]{1,0:T(8,128)(2,1)}, u32[]{:S(2)}, u32[]{:S(2)}) collective-permute-start(bf16[576,128]{1,0:T(8,128)(2,1)S(1)} %collective-permute-done.5.refs_2_), channel_id=1, source_target_pairs={{0,1},{1,0},{2,3},{3,2},{4,5},{5,4},{6,7},{7,6},{8,9},{9,8},{10,11... | collective-permute-start | bytes 442376 | tf_op jit(solution)/shard_map/ppermute | solution.py:322
  78.2 45.0 %all-to-all-start.2 = ((bf16[8,1408,128]{2,1,0:T(8,128)(2,1)}), bf16[8,1408,128]{2,1,0:T(8,128)(2,1)S(1)}, u32[]{:S(2)}, u32[]{:S(2)}) async-start(bf16[8,1408,128]{2,1,0:T(8,128)(2,1)} %get-tuple-element.29), calls=%async_computation.2 | async-start | bytes 5767168 | tf_op jit(solution)/shard_map/all_to_all | solution.py:345
  85.8 1.5 %collective-permute-start.11 = (bf16[576,128]{1,0:T(8,128)(2,1)S(1)}, bf16[576,128]{1,0:T(8,128)(2,1)S(1)}, u32[]{:S(2)}, u32[]{:S(2)}) collective-permute-start(bf16[576,128]{1,0:T(8,128)(2,1)S(1)} %get-tuple-element.34), channel_id=1, source_target_pairs={{0,1},{1,0},{2,3},{3,2},{4,5},{5,4},{6,7},{7,6},{8,9},{9,8},{10,11... | collective-permute-start | bytes 442376 | tf_op jit(solution)/shard_map/ppermute | solution.py:326
  87.3 7.2 %collective-permute-start.14 = (bf16[576,128]{1,0:T(8,128)(2,1)S(1)}, bf16[576,128]{1,0:T(8,128)(2,1)S(1)}, u32[]{:S(2)}, u32[]{:S(2)}) collective-permute-start(bf16[576,128]{1,0:T(8,128)(2,1)S(1)} %add_convert_fusion.2), channel_id=1, source_target_pairs={{6,0},{7,1},{0,2},{1,3},{2,4},{3,5},{4,6},{5,7},{14,8},{15,9},{8,1... | collective-permute-start | bytes 442376 | tf_op jit(solution)/shard_map/ppermute | solution.py:327
  88.8 8.1 %collective-permute-start.13 = (bf16[576,128]{1,0:T(8,128)(2,1)S(1)}, bf16[576,128]{1,0:T(8,128)(2,1)S(1)}, u32[]{:S(2)}, u32[]{:S(2)}) collective-permute-start(bf16[576,128]{1,0:T(8,128)(2,1)S(1)} %add_convert_fusion.2), channel_id=1, source_target_pairs={{2,0},{3,1},{4,2},{5,3},{6,4},{7,5},{0,6},{1,7},{10,8},{11,9},{12,... | collective-permute-start | bytes 442376 | tf_op jit(solution)/shard_map/ppermute | solution.py:327
  90.6 8.0 %collective-permute-start.12 = (bf16[576,128]{1,0:T(8,128)(2,1)S(1)}, bf16[576,128]{1,0:T(8,128)(2,1)S(1)}, u32[]{:S(2)}, u32[]{:S(2)}) collective-permute-start(bf16[576,128]{1,0:T(8,128)(2,1)S(1)} %add_convert_fusion.2), channel_id=1, source_target_pairs={{4,0},{5,1},{6,2},{7,3},{0,4},{1,5},{2,6},{3,7},{12,8},{13,9},{14,... | collective-permute-start | bytes 442376 | tf_op jit(solution)/shard_map/ppermute | solution.py:327
  98.7 20.4 %collective-permute-start.15 = (bf16[576,128]{1,0:T(8,128)(2,1)S(1)}, bf16[576,128]{1,0:T(8,128)(2,1)S(1)}, u32[]{:S(2)}, u32[]{:S(2)}) collective-permute-start(bf16[576,128]{1,0:T(8,128)(2,1)S(1)} %add_convert_fusion.1), channel_id=1, source_target_pairs={{0,8},{1,9},{2,10},{3,11},{4,12},{5,13},{6,14},{7,15},{8,0},{9,1},... | collective-permute-start | bytes 442376 | tf_op jit(solution)/shard_map/ppermute | solution.py:329
  119.1 1.5 %collective-permute-start.16 = (bf16[576,128]{1,0:T(8,128)(2,1)S(1)}, bf16[576,128]{1,0:T(8,128)(2,1)S(1)}, u32[]{:S(2)}, u32[]{:S(2)}) collective-permute-start(bf16[576,128]{1,0:T(8,128)(2,1)S(1)} %add_convert_fusion), channel_id=1, source_target_pairs={{0,1},{1,0},{2,3},{3,2},{4,5},{5,4},{6,7},{7,6},{8,9},{9,8},{10,11... | collective-permute-start | bytes 442376 | tf_op jit(solution)/shard_map/ppermute | solution.py:347
